TPU v7x, 128 devices: a whole 4x4x4 slice. The times are simulated.
128 devices in a mesh: dp: 4 (over y), expert: 32 (over z, x, core).
Axes of the slice: x: 4, y: 4, z: 4, core: 2. Of those that a mesh axis runs over, the one named last changes fastest.
Arguments:
- tokens: bfloat16 [16384, 7168], P(('dp', 'expert')), may hold values from -6 to 6
- grad_out: bfloat16 [16384, 7168], P(('dp', 'expert')), may hold values from -6 to 6
- routes: int32 [16384, 1], P(('dp', 'expert')), may hold values from 0 to 31; in each aligned block of 128 rows (0 to 127, 128 to 255, ...) at most 6 rows name the same one
- gate_prob: float32 [16384, 1], P(('dp', 'expert')), may hold values from 0.1 to 1
- w_gate: bfloat16 [32, 7168, 1024], P('expert', None, 'dp'), may hold values from -0.0625 to 0.0625
- w_up: bfloat16 [32, 7168, 1024], P('expert', None, 'dp'), may hold values from -0.0625 to 0.0625
- w_down: bfloat16 [32, 1024, 7168], P('expert', 'dp'), may hold values from -0.1875 to 0.1875
- moment_prev: float32 [32, 1024], P('expert', 'dp'), may hold values from 5 to 200
Outputs:
- grad_in: bfloat16 [16384, 7168], P(('dp', 'expert'))
- down_update: bfloat16 [32, 1024, 7168], P('expert', 'dp')
- second_moment: float32 [32, 1024], P('expert', 'dp')
Inputs may be any that keep to these rules, and one draw needn't show every extreme that they name: The 128 tokens of one device (aligned blocks of rows) name one expert in at most 6 routes; some block reaches 6.
All inputs are finite; a program needn't handle non-finite values.
Results may differ from a plain program's by a relative error of at most 0.0065.
Values may be sent and summed in bfloat16 or wider, within the bound.
A program may use at most 192 MiB of HBM per device.

v0:
```python
import jax
import jax.numpy as jnp
from jax import lax
from jax.sharding import PartitionSpec as P

moment_decay = 0.95
epsilon = 1e-08


def shards(tokens, grad_out, routes, gate_prob, w_gate, w_up, w_down, moment_prev):
    expert_count = lax.axis_size("expert")
    group_count = lax.axis_size("dp")
    token_count, model_width = tokens.shape
    top_count = routes.shape[1]
    route_count = token_count * top_count
    slot_cap = 3 * route_count // (2 * expert_count)
    buffer_rows = expert_count * slot_cap
    flat_expert = routes.reshape(route_count)
    onehot = (flat_expert[:, None] == jnp.arange(expert_count, dtype=jnp.int32)[None, :]).astype(
        jnp.int32
    )
    slot_index = jnp.sum((jnp.cumsum(onehot, axis=0) - onehot) * onehot, axis=1)
    position = flat_expert * slot_cap + slot_index
    route_rows = jnp.repeat(tokens, top_count, axis=0)
    scaled = jnp.repeat(grad_out, top_count, axis=0).astype(jnp.float32) * gate_prob
    route_cot = scaled.astype(jnp.bfloat16)
    selector = (position[:, None] == jnp.arange(buffer_rows, dtype=jnp.int32)[None, :]).astype(
        jnp.bfloat16
    )
    first_dims = (((0,), (0,)), ((), ()))
    last_dims = (((1,), (1,)), ((), ()))
    send_rows = lax.dot_general(
        selector, route_rows, first_dims, preferred_element_type=jnp.float32
    ).astype(jnp.bfloat16)
    send_cot = lax.dot_general(
        selector, route_cot, first_dims, preferred_element_type=jnp.float32
    ).astype(jnp.bfloat16)
    shape_all = (group_count * buffer_rows, model_width)
    copies_rows = jnp.broadcast_to(
        send_rows[None], (group_count, buffer_rows, model_width)
    ).reshape(shape_all)
    copies_cot = jnp.broadcast_to(send_cot[None], (group_count, buffer_rows, model_width)).reshape(
        shape_all
    )
    rows_in, cot_in = (
        lax.all_to_all(copies_rows, ("dp", "expert"), split_axis=0, concat_axis=0, tiled=True),
        lax.all_to_all(copies_cot, ("dp", "expert"), split_axis=0, concat_axis=0, tiled=True),
    )
    gate_w = w_gate[0]
    up_w = w_up[0]
    down_w = w_down[0]
    gate_pre = jnp.dot(rows_in, gate_w, preferred_element_type=jnp.float32)
    up_pre = jnp.dot(rows_in, up_w, preferred_element_type=jnp.float32)
    gate_sig = jax.nn.sigmoid(gate_pre)
    silu_gate = gate_pre * gate_sig
    hidden = (silu_gate * up_pre).astype(jnp.bfloat16)
    hidden_grad = lax.dot_general(cot_in, down_w, last_dims, preferred_element_type=jnp.float32)
    gate_grad = (hidden_grad * up_pre * gate_sig * (1.0 + gate_pre * (1.0 - gate_sig))).astype(
        jnp.bfloat16
    )
    up_grad = (hidden_grad * silu_gate).astype(jnp.bfloat16)
    partial_value = lax.dot_general(
        gate_grad, gate_w, last_dims, preferred_element_type=jnp.float32
    )
    partial_value = (
        partial_value
        + lax.dot_general(up_grad, up_w, last_dims, preferred_element_type=jnp.float32)
    ).astype(jnp.bfloat16)
    returned = lax.all_to_all(
        partial_value, ("dp", "expert"), split_axis=0, concat_axis=0, tiled=True
    )
    summed = jnp.sum(
        returned.reshape(group_count, buffer_rows, model_width).astype(jnp.float32), axis=0
    )
    route_grad = jnp.take(summed, position, axis=0)
    grad_in = jnp.sum(route_grad.reshape(token_count, top_count, model_width), axis=1).astype(
        jnp.bfloat16
    )
    down_wgrad = lax.dot_general(hidden, cot_in, first_dims, preferred_element_type=jnp.float32)
    gate_wgrad = lax.dot_general(rows_in, gate_grad, first_dims, preferred_element_type=jnp.float32)
    up_wgrad = lax.dot_general(rows_in, up_grad, first_dims, preferred_element_type=jnp.float32)
    mean_square = (
        jnp.sum(gate_wgrad * gate_wgrad, axis=0)
        + jnp.sum(up_wgrad * up_wgrad, axis=0)
        + jnp.sum(down_wgrad * down_wgrad, axis=1)
    ) / (3.0 * model_width)
    second_moment = moment_decay * moment_prev[0] + (1.0 - moment_decay) * mean_square
    down_update = (down_wgrad / (jnp.sqrt(second_moment)[:, None] + epsilon)).astype(jnp.bfloat16)
    return (grad_in, down_update[None], second_moment[None])


def solution(mesh):
    placed = (
        P(("dp", "expert"), None),
        P(("dp", "expert"), None),
        P(("dp", "expert"), None),
        P(("dp", "expert"), None),
        P("expert", None, "dp"),
        P("expert", None, "dp"),
        P("expert", "dp", None),
        P("expert", "dp"),
    )
    return jax.shard_map(
        shards,
        mesh=mesh,
        in_specs=placed,
        out_specs=(P(("dp", "expert"), None), P("expert", "dp", None), P("expert", "dp")),
        check_vma=False,
    )
```

profile of v0, /device:TPU:74, one launch (start us, length us, event | category | flops | bytes accessed | tf_op | source)
XLA Modules:
  0.0 763.0 jit_solution(15197129525399336257)
XLA Ops:
  0.6 0.0 copy-start
  0.6 0.9 fusion.18
  1.5 0.2 reduce_window_sum.11
  1.7 0.8 select_reduce_fusion
  2.5 0.7 fusion.20
  3.2 0.0 copy-done
  3.2 2.5 convolution_convert_fusion
  5.7 7.3 broadcast_in_dim.35
  13.0 15.2 %all_to_all.25 = bf16[128,6,7168]{2,1,0:T(8,128)(2,1)} reshape(bf16[4,192,7168]{2,1,0:T(8,128)(2,1)} %broadcast_in_dim.35) | data formatting | bytes 22020096 | tf_op jit(solution)/shard_map/all_to_all | solution.py:46
  28.3 10.4 %all-to-all-start.1 = ((bf16[128,6,7168]{2,1,0:T(8,128)(2,1)}), bf16[128,6,7168]{2,1,0:T(8,128)(2,1)}, u32[]{:S(2)}, u32[]{:S(2)}) async-start(bf16[128,6,7168]{2,1,0:T(8,128)(2,1)} %all_to_all.25), calls=%async_computation.1 | async-start | bytes 29360128 | tf_op jit(solution)/shard_map/all_to_all | solution.py:46
  38.7 0.0 copy-done.5
  38.7 0.0 copy-done.8
  38.7 2.5 convolution_convert_fusion.1
  41.2 7.3 broadcast_in_dim.34
  48.6 16.0 %all_to_all.22 = bf16[128,6,7168]{2,1,0:T(8,128)(2,1)} reshape(bf16[4,192,7168]{2,1,0:T(8,128)(2,1)} %broadcast_in_dim.34) | data formatting | bytes 22020096 | tf_op jit(solution)/shard_map/all_to_all | solution.py:47
  64.5 174.4 %all-to-all-done.1 = bf16[128,6,7168]{2,1,0:T(8,128)(2,1)} async-done(((bf16[128,6,7168]{2,1,0:T(8,128)(2,1)}), bf16[128,6,7168]{2,1,0:T(8,128)(2,1)}, u32[]{:S(2)}, u32[]{:S(2)}) %all-to-all-start.1) | async-done | bytes 11010080 | tf_op jit(solution)/shard_map/all_to_all | solution.py:46
  239.0 7.1 all-to-all-start
  246.0 16.5 %all_to_all.27 = bf16[768,7168]{1,0:T(8,128)(2,1)} reshape(bf16[128,6,7168]{2,1,0:T(8,128)(2,1)} %all-to-all-done.1) | data formatting | bytes 22020096 | tf_op jit(solution)/shard_map/all_to_all | solution.py:46
  262.5 7.0 fusion.2
  269.6 1.3 copy-done.2
  270.9 1.0 copy-done.3
  271.9 3.0 fusion.5
  274.9 173.0 %all-to-all-done = bf16[128,6,7168]{2,1,0:T(8,128)(2,1)} async-done(((bf16[128,6,7168]{2,1,0:T(8,128)(2,1)}), bf16[128,6,7168]{2,1,0:T(8,128)(2,1)}, u32[]{:S(2)}, u32[]{:S(2)}) %all-to-all-start) | async-done | bytes 11010080 | tf_op jit(solution)/shard_map/all_to_all | solution.py:47
  448.0 16.4 %all_to_all.24 = bf16[768,7168]{1,0:T(8,128)(2,1)} reshape(bf16[128,6,7168]{2,1,0:T(8,128)(2,1)} %all-to-all-done) | data formatting | bytes 22020096 | tf_op jit(solution)/shard_map/all_to_all | solution.py:47
  464.4 8.5 %multiply_convert_fusion.3 = (bf16[768,256]{1,0:T(8,128)(2,1)S(1)}, bf16[768,256]{1,0:T(8,128)(2,1)S(1)}) fusion(f32[768,256]{1,0:T(8,128)S(1)} %fusion.2, f32[768,256]{1,0:T(8,128)S(1)} %fusion.5, bf16[768,7168]{1,0:T(8,128)(2,1)} %all_to_all.24, bf16[1,256,7168]{2,1,0:T(8,128)(2,1)} %param.14), kind=kOutput, calls=%fused_computation.24 | convolution fusion | flops 2821128192 | bytes 17039360 | tf_op jit(solution)/shard_map/dot_general | solution.py:57
  472.9 0.0 copy-done.4
  472.9 9.1 %fusion = f32[768,7168]{1,0:T(8,128)} fusion(bf16[768,256]{1,0:T(8,128)(2,1)S(1)} %get-tuple-element.6, bf16[1,7168,256]{2,1,0:T(8,128)(2,1)S(1)} %copy-done.4), kind=kOutput, calls=%fused_computation.8 | convolution fusion | flops 2818572288 | bytes 26083328 | tf_op jit(solution)/shard_map/dot_general | solution.py:62
  482.0 13.5 %add_convert_fusion = bf16[768,7168]{1,0:T(8,128)(2,1)} fusion(f32[768,7168]{1,0:T(8,128)} %fusion, bf16[768,256]{1,0:T(8,128)(2,1)S(1)} %get-tuple-element.5, bf16[1,7168,256]{2,1,0:T(8,128)(2,1)} %param.13), kind=kOutput, calls=%fused_computation.1 | convolution fusion | flops 2829582336 | bytes 37093376 | tf_op jit(solution)/shard_map/dot_general | solution.py:67
  495.5 15.1 %all_to_all.28 = bf16[128,6,7168]{2,1,0:T(8,128)(2,1)} reshape(bf16[768,7168]{1,0:T(8,128)(2,1)} %add_convert_fusion) | data formatting | bytes 22020096 | tf_op jit(solution)/shard_map/all_to_all | solution.py:69
  510.7 7.1 all-to-all-start.2
  517.8 0.0 copy-done.6
  517.8 0.0 copy-done.7
  517.8 0.0 slice-start
  517.8 0.0 slice-start.1
  517.8 6.2 multiply_reduce_fusion
  524.1 0.0 slice-start.2
  524.1 7.4 fusion.11
  531.5 0.0 slice-done
  531.5 0.0 slice-done.1
  531.5 0.0 slice-done.2
  531.5 3.4 fusion.10
  535.0 0.6 fusion.21
  535.5 2.6 fusion.9
  538.2 186.2 %all-to-all-done.2 = bf16[128,6,7168]{2,1,0:T(8,128)(2,1)} async-done(((bf16[128,6,7168]{2,1,0:T(8,128)(2,1)}), bf16[128,6,7168]{2,1,0:T(8,128)(2,1)}, u32[]{:S(2)}, u32[]{:S(2)}) %all-to-all-start.2) | async-done | bytes 11010080 | tf_op jit(solution)/shard_map/all_to_all | solution.py:69
  724.3 17.8 %reshape.84 = f32[4,192,7168]{2,1,0:T(8,128)} reshape(bf16[128,6,7168]{2,1,0:T(8,128)(2,1)} %all-to-all-done.2) | data formatting | bytes 33030144 | tf_op jit(solution)/shard_map/convert_element_type | solution.py:73
  742.1 10.8 %reduce_sum.53 = bf16[192,7168]{1,0:T(8,128)(2,1)} reduce(f32[4,192,7168]{2,1,0:T(8,128)} %reshape.84, f32[]{:T(128)} %constant.31.clone.1), dimensions={0}, to_apply=%region_2.3 | reduce | flops 4128768 | bytes 24772612 | tf_op jit(solution)/shard_map/reduce_sum | solution.py:72
  753.0 6.9 gather_fusion
  759.8 3.1 select_convert_fusion
  (14 shorter events, 0.0 us)
Async XLA Ops:
  0.6 2.6 copy-start
  28.3 10.4 %copy-start.5 = (bf16[128,7168]{1,0:T(8,128)(2,1)S(1)}, bf16[128,7168]{1,0:T(8,128)(2,1)}, u32[]{:S(2)}) copy-start(bf16[128,7168]{1,0:T(8,128)(2,1)} %param.9) | copy-start | bytes 5505028
  28.3 10.4 %copy-start.8 = (f32[128,1]{0,1:T(1,128)S(1)}, f32[128,1]{0,1:T(1,128)}, u32[]{:S(2)}) copy-start(f32[128,1]{0,1:T(1,128)} %param.11) | copy-start | bytes 1540
  28.3 210.7 %all-to-all-start.1 = ((bf16[128,6,7168]{2,1,0:T(8,128)(2,1)}), bf16[128,6,7168]{2,1,0:T(8,128)(2,1)}, u32[]{:S(2)}, u32[]{:S(2)}) async-start(bf16[128,6,7168]{2,1,0:T(8,128)(2,1)} %all_to_all.25), calls=%async_computation.1 | async-start | bytes 29360128 | tf_op jit(solution)/shard_map/all_to_all | solution.py:46
  239.0 209.0 %all-to-all-start = ((bf16[128,6,7168]{2,1,0:T(8,128)(2,1)}), bf16[128,6,7168]{2,1,0:T(8,128)(2,1)}, u32[]{:S(2)}, u32[]{:S(2)}) async-start(bf16[128,6,7168]{2,1,0:T(8,128)(2,1)} %all_to_all.22), calls=%async_computation | async-start | bytes 29360128 | tf_op jit(solution)/shard_map/all_to_all | solution.py:47
  262.5 8.4 %copy-start.2 = (bf16[768,7168]{1,0:T(8,128)(2,1)S(1)}, bf16[768,7168]{1,0:T(8,128)(2,1)}, u32[]{:S(2)}) copy-start(bf16[768,7168]{1,0:T(8,128)(2,1)} %all_to_all.27) | copy-start | bytes 33030148
  262.5 9.4 %copy-start.3 = (bf16[1,7168,256]{2,1,0:T(8,128)(2,1)S(1)}, bf16[1,7168,256]{2,1,0:T(8,128)(2,1)}, u32[]{:S(2)}) copy-start(bf16[1,7168,256]{2,1,0:T(8,128)(2,1)} %param.13) | copy-start | bytes 11010052
  464.4 8.5 %copy-start.4 = (bf16[1,7168,256]{2,1,0:T(8,128)(2,1)S(1)}, bf16[1,7168,256]{2,1,0:T(8,128)(2,1)}, u32[]{:S(2)}) copy-start(bf16[1,7168,256]{2,1,0:T(8,128)(2,1)} %param.12) | copy-start | bytes 11010052
  510.7 7.1 copy-start.6
  510.7 7.1 copy-start.7
  510.7 213.6 %all-to-all-start.2 = ((bf16[128,6,7168]{2,1,0:T(8,128)(2,1)}), bf16[128,6,7168]{2,1,0:T(8,128)(2,1)}, u32[]{:S(2)}, u32[]{:S(2)}) async-start(bf16[128,6,7168]{2,1,0:T(8,128)(2,1)} %all_to_all.28), calls=%async_computation.2 | async-start | bytes 29360128 | tf_op jit(solution)/shard_map/all_to_all | solution.py:69
  517.8 13.6 %slice-start = ((s8[11010048]{0:T(1024)(128)(4,1)}), s8[4194304]{0:T(1024)(128)(4,1)S(1)}, s32[]{:S(2)}) async-start(s8[11010048]{0:T(1024)(128)(4,1)} %bitcast.46), calls=%async_computation.3 | async-start | bytes 8388608
  517.8 13.6 %slice-start.1 = ((s8[11010048]{0:T(1024)(128)(4,1)}), s8[4194304]{0:T(1024)(128)(4,1)S(1)}, s32[]{:S(2)}) async-start(s8[11010048]{0:T(1024)(128)(4,1)} %bitcast.46), calls=%async_computation.4 | async-start | bytes 8388608
  524.1 7.4 slice-start.2
  752.9 10.0 %copy-start.1 = (bf16[128,7168]{1,0:T(8,128)(2,1)S(1)}, bf16[128,7168]{1,0:T(8,128)(2,1)}, u32[]{:S(2)}) copy-start(bf16[128,7168]{1,0:T(8,128)(2,1)} %param.8) | copy-start | bytes 5505028
where the time goes:
time: 766 us; the launch traced here: 763 us
  waiting for transfers between devices  534 us (70%)
  local copies, waits for them, and re-layouts  121 us (16%)
  matrix products  63.3 us (8%)
  starting transfers between devices  24.5 us (3%)
  other arithmetic  19.7 us (3%)
    all_to_all x1, waiting for transfers between devices, shards(): lax.all_to_all(partial_value, ('dp', 'expert'), split_axis=0, concat_axis...  186 us
    all_to_all x1, waiting for transfers between devices, shards(): lax.all_to_all(copies_rows, ('dp', 'expert'), split_axis=0, concat_axis=0...  174 us
    all_to_all x1, waiting for transfers between devices, shards(): lax.all_to_all(copies_cot, ('dp', 'expert'), split_axis=0, concat_axis=0,...  173 us
    all_to_all x2, local copies, waits for them, and re-layouts, shards(): lax.all_to_all(copies_cot, ('dp', 'expert'), split_axis=0, concat_axis=0,...  32.4 us
    all_to_all x2, local copies, waits for them, and re-layouts, shards(): lax.all_to_all(copies_rows, ('dp', 'expert'), split_axis=0, concat_axis=0...  31.7 us
    convert_element_type x1, local copies, waits for them, and re-layouts, shards(): returned.reshape(group_count, buffer_rows, model_width).astype(jnp.float32)  17.8 us
  transfers between devices with their start and end apart: 3, of which 3 were waited for; matrix products, arithmetic and copies ran while one was open for 5% of the time, Pallas kernels for 0%

commit v1 on v0

v1 whole, which is shorter than its diff:
```python
import functools

import jax
import jax.numpy as jnp
from jax import lax
from jax.experimental import pallas as pl
from jax.experimental.pallas import tpu as pltpu
from jax.sharding import PartitionSpec as P

MESH = pl.DeviceIdType.MESH
BF = jnp.bfloat16
F32 = jnp.float32

moment_decay = 0.95
epsilon = 1e-08

D = 7168
TOK = 128
CAP = 6
Q = 256
ROWS = 192
HALF = 96
BLK = 48
CW = 1024
NCH = D // CW
SUB = 256
PARTNERS = (
    (0, 0, 0, 1),
    (0, 1, 0, 0),
    (0, 2, 0, 0),
    (0, 3, 0, 0),
    (0, 0, 1, 0),
    (0, 0, 2, 0),
    (0, 0, 3, 0),
    (1, 0, 0, 0),
    (3, 0, 0, 0),
)


def place():
    y = lax.axis_index("dp")
    e = lax.axis_index("expert")
    return y, e // 8, (e // 2) % 4, e % 2


def peer(here, dy, dz, dx, dc):
    y, z, x, c = here
    expert = (((z + dz) % 4) * 4 + (x + dx) % 4) * 2 + (c + dc) % 2
    return {"dp": (y + dy) % 4, "expert": expert}


def remote(src, dst, send, recv, device):
    return pltpu.make_async_remote_copy(
        src_ref=src,
        dst_ref=dst,
        send_sem=send,
        recv_sem=recv,
        device_id=device,
        device_id_type=MESH,
    )


def greet(here):
    barrier = pltpu.get_barrier_semaphore()
    for offset in PARTNERS:
        pl.semaphore_signal(barrier, inc=1, device_id=peer(here, *offset), device_id_type=MESH)
    pl.semaphore_wait(barrier, len(PARTNERS))


def at(index, size, align):
    return pl.ds(pl.multiple_of(index * size, align), size)


def cols(k):
    return at(k, CW, 128)


def tile(k, j):
    return pl.ds(pl.multiple_of(k * CW + j * SUB, 128), SUB)


def nt(a, b):
    return lax.dot_general(a, b, (((1,), (1,)), ((), ())), preferred_element_type=F32)


def tn(a, b):
    return lax.dot_general(a, b, (((0,), (0,)), ((), ())), preferred_element_type=F32)


def nn(a, b):
    return jnp.dot(a, b, preferred_element_type=F32)


def forward_kernel(
    meta_ref,
    perm_ref,
    tok_ref,
    cot_ref,
    wg_hbm,
    wu_hbm,
    wd_hbm,
    rows,
    acts,
    acts_t,
    sel_ref,
    metas,
    gp_ref,
    raw,
    zs,
    za,
    xs,
    stage,
    acc,
    wg,
    wu,
    wd,
    w_sem,
    m_sem,
    raw_l,
    raw_s,
    raw_r,
    z_s,
    z_r,
    x_s,
    x_r,
    x_l,
    y_s,
    y_r,
    f_s,
    f_r,
    st_l,
):
    here = place()
    y, z, x, c = here
    sources = (tok_ref, cot_ref)
    greet(here)

    meta_copy = remote(meta_ref, metas.at[c], m_sem.at[0], m_sem.at[1], peer(here, 0, 0, 0, 1))
    meta_copy.start()
    metas[pl.ds(c, 1)] = meta_ref[...][None]

    def raw_local(a, k):
        return pltpu.make_async_copy(
            sources[a].at[:, cols(k)], raw.at[a, at(c, TOK, TOK), cols(k)], raw_l.at[a, k]
        )

    def raw_remote(a, k):
        return remote(
            sources[a].at[:, cols(k)],
            raw.at[a, at(c, TOK, TOK), cols(k)],
            raw_s.at[a, k],
            raw_r.at[a, k],
            peer(here, 0, 0, 0, 1),
        )

    for k in range(NCH):
        for a in range(2):
            raw_local(a, k).start()
            raw_remote(a, k).start()
    weights = [
        pltpu.make_async_copy(src, dst, w_sem.at[i])
        for i, (src, dst) in enumerate(((wg_hbm, wg), (wu_hbm, wu), (wd_hbm, wd)))
    ]
    for copy in weights:
        copy.start()

    acc[...] = jnp.zeros_like(acc)
    meta_copy.wait()

    earlier = (
        lax.broadcasted_iota(jnp.int32, (TOK, TOK), 0)
        < lax.broadcasted_iota(jnp.int32, (TOK, TOK), 1)
    ).astype(F32).astype(BF)
    gp = jnp.zeros((ROWS, 1), F32)
    for m in range(2):
        route = metas[m, 0:1, :].astype(jnp.int32)
        prob = metas[m, 1:2, :]
        onehot = (lax.broadcasted_iota(jnp.int32, (32, TOK), 0) == route).astype(F32)
        before = nn(onehot.astype(BF), earlier)
        slot = jnp.sum(onehot * before, axis=0, keepdims=True).astype(jnp.int32)
        row = ((route >> 1) * 2 + m) * CAP + slot
        row = jnp.where((route & 1) == c, row, -1)
        chosen = lax.broadcasted_iota(jnp.int32, (ROWS, TOK), 0) == row
        sel_ref[:, m * TOK : (m + 1) * TOK] = chosen.astype(F32).astype(BF)
        gp = gp + jnp.sum(jnp.where(chosen, prob, 0.0), axis=1, keepdims=True)
    gp_ref[...] = jnp.broadcast_to(gp, (ROWS, 128))

    def z_copy(a, k, d):
        return remote(
            zs.at[a, k % 2, at((z + d) % 4, BLK, 16), :],
            za.at[a, at(z, BLK, 16), cols(k)],
            z_s.at[a, k % 2, d - 1],
            z_r.at[a, k, d - 1],
            peer(here, 0, d, 0, 0),
        )

    def x_copy(a, k, d):
        return remote(
            xs.at[a, k % 2, at((x + d) % 4, BLK, 16), :],
            rows.at[a, y, at(x, BLK, 16), cols(k)],
            x_s.at[a, k % 2, d - 1],
            x_r.at[a, k, d - 1],
            peer(here, 0, 0, d, 0),
        )

    def x_own(a, k):
        return pltpu.make_async_copy(
            xs.at[a, k % 2, at(x, BLK, 16), :],
            rows.at[a, y, at(x, BLK, 16), cols(k)],
            x_l.at[a, k % 2],
        )

    def y_copy(a, k, i):
        return remote(
            rows.at[a, y, :, cols(k)],
            rows.at[a, y, :, cols(k)],
            y_s.at[a, k, i],
            y_r.at[a, k, i],
            peer(here, 1 if i == 0 else 3, 0, 0, 0),
        )

    def f_copy(a, k, i):
        src = (y + (3 if i == 0 else 1)) % 4
        half = rows.at[a, src, pl.ds(i * HALF, HALF), cols(k)]
        return remote(
            half, half, f_s.at[a, k, i], f_r.at[a, k, i], peer(here, 1 if i == 0 else 3, 0, 0, 0)
        )

    def stage_copy(a, k):
        return pltpu.make_async_copy(
            rows.at[a, :, :, cols(k)], stage.at[a, k % 2], st_l.at[a, k % 2]
        )

    def when(k, body):
        pl.when((k >= 0) & (k < NCH))(lambda: body(k))

    def drain(copy, count, first):
        def body(k):
            for a in range(2):
                for i in range(count):
                    copy(a, k, first + i).wait_send()

        return body

    def select(k):
        for a in range(2):
            raw_local(a, k).wait()
            raw_remote(a, k).wait()
            for j in range(CW // SUB):
                picked = nn(sel_ref[...], raw[a, :, tile(k, j)])
                if a == 1:
                    picked = picked * gp_ref[:, 0:1]
                zs[a, k % 2, :, j * SUB : (j + 1) * SUB] = picked.astype(BF)
            for d in (2, 1, 3):
                z_copy(a, k, d).start()
            za[a, at(z, BLK, 16), cols(k)] = zs[a, k % 2, at(z, BLK, 16), :]

    def turn(k):
        for a in range(2):
            for d in (1, 2, 3):
                z_copy(a, k, d).wait_recv()
            for j in range(CW // SUB):
                xs[a, k % 2, :, j * SUB : (j + 1) * SUB] = nn(
                    perm_ref[...], za[a, :, tile(k, j)]
                ).astype(BF)
            for d in (2, 1, 3):
                x_copy(a, k, d).start()
            x_own(a, k).start()

    def spread(k):
        for a in range(2):
            for d in (1, 2, 3):
                x_copy(a, k, d).wait_recv()
            x_own(a, k).wait()
            for i in range(2):
                y_copy(a, k, i).start()

    def pass_on(k):
        for a in range(2):
            for i in range(2):
                y_copy(a, k, i).wait_recv()
                f_copy(a, k, i).start()

    def fetch(k):
        for a in range(2):
            for i in range(2):
                f_copy(a, k, i).wait_recv()
            stage_copy(a, k).start()

    def accumulate(k):
        @pl.when(k == 0)
        def _():
            for copy in weights:
                copy.wait()

        for a in range(2):
            stage_copy(a, k).wait()

        def block(b, carry):
            block_rows = at(b, ROWS, 16)
            tokens = stage[0, k % 2, b]
            acc[0, block_rows, :] += nn(tokens, wg[cols(k), :])
            acc[1, block_rows, :] += nn(tokens, wu[cols(k), :])
            acc[2, block_rows, :] += nt(stage[1, k % 2, b], wd[:, cols(k)])
            return carry

        lax.fori_loop(0, 4, block, 0)

    def step(t, carry):
        when(t - 2, drain(z_copy, 3, 1))
        when(t - 3, drain(x_copy, 3, 1))
        when(t - 4, drain(y_copy, 2, 0))
        when(t - 5, drain(f_copy, 2, 0))
        when(t, select)
        when(t - 1, turn)
        when(t - 2, spread)
        when(t - 3, pass_on)
        when(t - 4, fetch)
        when(t - 5, accumulate)
        return carry

    lax.fori_loop(0, NCH + 5, step, 0)

    def finish(b, carry):
        part = at(b, Q, 256)
        gate, up, grad = acc[0, part, :], acc[1, part, :], acc[2, part, :]
        sig = jax.nn.sigmoid(gate)
        silu = gate * sig
        hidden = silu * up
        gate_grad = grad * up * sig * (1.0 + gate * (1.0 - sig))
        up_grad = grad * silu
        acts[0, part, :] = gate_grad.astype(BF)
        acts[1, part, :] = up_grad.astype(BF)
        acts_t[0, :, part] = hidden.T.astype(BF)
        acts_t[1, :, part] = gate_grad.T.astype(BF)
        acts_t[2, :, part] = up_grad.T.astype(BF)
        return carry

    lax.fori_loop(0, 3, finish, 0)


def backward_kernel(
    acts,
    acts_t,
    sel_ref,
    perm_ref,
    rows,
    wg_hbm,
    wu_hbm,
    moment_ref,
    grad_ref,
    update_ref,
    second_ref,
    far,
    relay,
    near,
    summed,
    xs,
    xa,
    zs,
    za,
    cs,
    co,
    cr,
    stage,
    dw,
    squares,
    wg,
    wu,
    w_sem,
    p_s,
    p_r,
    n_s,
    n_r,
    x_s,
    x_r,
    z_s,
    z_r,
    c_s,
    c_r,
    st_l,
):
    here = place()
    y, z, x, c = here
    greet(here)
    weights = [
        pltpu.make_async_copy(src, dst, w_sem.at[i])
        for i, (src, dst) in enumerate(((wg_hbm, wg), (wu_hbm, wu)))
    ]
    for copy in weights:
        copy.start()

    def stage_copy(a, k):
        return pltpu.make_async_copy(
            rows.at[a, :, :, cols(k)], stage.at[a, k % 2], st_l.at[a, k % 2]
        )

    for a in range(2):
        stage_copy(a, 0).start()
    squares[...] = jnp.zeros_like(squares)
    for copy in weights:
        copy.wait()

    def partial(block, k, j):
        block_rows = at(block, ROWS, 16)
        total = nt(acts[0, block_rows, :], wg[tile(k, j), :])
        total = total + nt(acts[1, block_rows, :], wu[tile(k, j), :])
        return total.astype(BF).astype(F32)

    def p_copy(k, i):
        return remote(
            far.at[k % 2, pl.ds(i * HALF, HALF), :],
            relay.at[i, :, cols(k)],
            p_s.at[k % 2, i],
            p_r.at[k, i],
            peer(here, 1 if i == 0 else 3, 0, 0, 0),
        )

    def n_copy(k, i):
        return remote(
            near.at[i, k % 2],
            summed.at[i, :, cols(k)],
            n_s.at[k % 2, i],
            n_r.at[k, i],
            peer(here, 1 if i == 0 else 3, 0, 0, 0),
        )

    def x_copy(k, d):
        return remote(
            xs.at[k % 2, at((x + d) % 4, BLK, 16), :],
            xa.at[at(x, BLK, 16), cols(k)],
            x_s.at[k % 2, d - 1],
            x_r.at[k, d - 1],
            peer(here, 0, 0, d, 0),
        )

    def z_copy(k, d):
        return remote(
            zs.at[k % 2, at((z + d) % 4, BLK, 16), :],
            za.at[at(z, BLK, 16), cols(k)],
            z_s.at[k % 2, d - 1],
            z_r.at[k, d - 1],
            peer(here, 0, d, 0, 0),
        )

    def c_copy(k):
        return remote(
            cs.at[k % 2], cr.at[:, cols(k)], c_s.at[k % 2], c_r.at[k], peer(here, 0, 0, 0, 1)
        )

    def when(k, body):
        pl.when((k >= 0) & (k < NCH))(lambda: body(k))

    def drain(copy, count, first):
        def body(k):
            for i in range(count):
                copy(k, first + i).wait_send()

        return body

    def send_far(k):
        for j in range(CW // SUB):
            far[k % 2, :, j * SUB : (j + 1) * SUB] = partial((y + 2) % 4, k, j).astype(BF)
        for i in range(2):
            p_copy(k, i).start()

    def send_near(k):
        for i in range(2):
            p_copy(k, i).wait_recv()
            for j in range(CW // SUB):
                out = pl.ds(j * SUB, SUB)
                term = partial((y + (1 if i == 0 else 3)) % 4, k, j)
                arrived = relay[i, :, tile(k, j)].astype(F32)
                if i == 0:
                    near[i, k % 2, 0:HALF, out] = (term[0:HALF] + arrived).astype(BF)
                    near[i, k % 2, HALF:ROWS, out] = term[HALF:ROWS].astype(BF)
                else:
                    near[i, k % 2, 0:HALF, out] = term[0:HALF].astype(BF)
                    near[i, k % 2, HALF:ROWS, out] = (term[HALF:ROWS] + arrived).astype(BF)
            n_copy(k, i).start()

    def total(k):
        for i in range(2):
            n_copy(k, i).wait_recv()
        for j in range(CW // SUB):
            whole = partial(y, k, j)
            whole = whole + summed[0, :, tile(k, j)].astype(F32)
            whole = whole + summed[1, :, tile(k, j)].astype(F32)
            xs[k % 2, :, j * SUB : (j + 1) * SUB] = whole.astype(BF)
        for d in (2, 1, 3):
            x_copy(k, d).start()
        xa[at(x, BLK, 16), cols(k)] = xs[k % 2, at(x, BLK, 16), :]

    def turn(k):
        for d in (1, 2, 3):
            x_copy(k, d).wait_recv()
        for j in range(CW // SUB):
            zs[k % 2, :, j * SUB : (j + 1) * SUB] = nn(perm_ref[...], xa[:, tile(k, j)]).astype(BF)
        for d in (2, 1, 3):
            z_copy(k, d).start()
        za[at(z, BLK, 16), cols(k)] = zs[k % 2, at(z, BLK, 16), :]

    def unselect(k):
        for d in (1, 2, 3):
            z_copy(k, d).wait_recv()
        for j in range(CW // SUB):
            out = pl.ds(j * SUB, SUB)
            block = za[:, tile(k, j)]
            cs[k % 2, :, out] = tn(sel_ref[:, at(1 - c, TOK, TOK)], block).astype(BF)
            co[k % 2, :, out] = tn(sel_ref[:, at(c, TOK, TOK)], block).astype(BF)
        c_copy(k).start()

    def join(k):
        c_copy(k).wait()
        mine = co[k % 2].astype(F32) + cr[:, cols(k)].astype(F32)
        grad_ref[:, cols(k)] = mine.astype(BF)

    def weight_grads(k):
        for a in range(2):
            stage_copy(a, k).wait()

        @pl.when(k + 1 < NCH)
        def _():
            for a in range(2):
                stage_copy(a, k + 1).start()

        for j in range(CW // SUB):
            out = slice(j * SUB, (j + 1) * SUB)
            cot_rows = stage[1, k % 2, :, :, out].reshape(4 * ROWS, SUB)
            tok_rows = stage[0, k % 2, :, :, out].reshape(4 * ROWS, SUB)
            down = nn(acts_t[0], cot_rows)
            dw[:, tile(k, j)] = down
            gate = nn(acts_t[1], tok_rows)
            up = nn(acts_t[2], tok_rows)
            sq = down * down + gate * gate + up * up
            squares[...] += sq[:, 0:128] + sq[:, 128:256]

    def update(k):
        @pl.when(k == 0)
        def _():
            mean = jnp.sum(squares[...], axis=1, keepdims=True) / (3.0 * D)
            second = moment_decay * moment_ref[...] + (1.0 - moment_decay) * mean
            second_ref[...] = second
            squares[...] = jnp.broadcast_to(1.0 / (jnp.sqrt(second) + epsilon), squares.shape)

        for j in range(CW // 128):
            out = pl.ds(pl.multiple_of(k * CW + j * 128, 128), 128)
            update_ref[:, out] = (dw[:, out] * squares[...]).astype(BF)

    def step(t, carry):
        when(t - 2, drain(p_copy, 2, 0))
        when(t - 3, drain(n_copy, 2, 0))
        when(t - 4, drain(x_copy, 3, 1))
        when(t - 5, drain(z_copy, 3, 1))
        when(t, send_far)
        when(t - 1, send_near)
        when(t - 2, total)
        when(t - 3, turn)
        when(t - 4, unselect)
        when(t - 5, join)
        when(t, weight_grads)
        when((t - NCH) * 2, update)
        when((t - NCH) * 2 + 1, update)
        return carry

    lax.fori_loop(0, NCH + 5, step, 0)


def shards(tokens, grad_out, routes, gate_prob, w_gate, w_up, w_down, moment_prev):
    meta = jnp.concatenate(
        [routes.reshape(1, TOK).astype(F32), gate_prob.reshape(1, TOK), jnp.zeros((6, TOK), F32)]
    )
    index = jnp.arange(ROWS)
    swapped = (index % BLK) // 12 * BLK + index // BLK * 12 + index % 12
    perm = (swapped[:, None] == index[None, :]).astype(BF)
    vmem = pl.BlockSpec(memory_space=pltpu.VMEM)
    hbm = pl.BlockSpec(memory_space=pltpu.HBM)
    dma = pltpu.SemaphoreType.DMA
    rows, acts, acts_t, sel = pl.pallas_call(
        forward_kernel,
        name="dispatch",
        out_shape=(
            jax.ShapeDtypeStruct((2, 4, ROWS, D), BF),
            jax.ShapeDtypeStruct((2, 4 * ROWS, Q), BF),
            jax.ShapeDtypeStruct((3, Q, 4 * ROWS), BF),
            jax.ShapeDtypeStruct((ROWS, 2 * TOK), BF),
        ),
        in_specs=[vmem, vmem, hbm, hbm, hbm, hbm, hbm],
        out_specs=(hbm, vmem, vmem, vmem),
        scratch_shapes=[
            pltpu.VMEM((2, 8, TOK), F32),
            pltpu.VMEM((ROWS, 128), F32),
            pltpu.VMEM((2, 2 * TOK, D), BF),
            pltpu.VMEM((2, 2, ROWS, CW), BF),
            pltpu.VMEM((2, ROWS, D), BF),
            pltpu.VMEM((2, 2, ROWS, CW), BF),
            pltpu.VMEM((2, 2, 4, ROWS, CW), BF),
            pltpu.VMEM((3, 4 * ROWS, Q), F32),
            pltpu.VMEM((D, Q), BF),
            pltpu.VMEM((D, Q), BF),
            pltpu.VMEM((Q, D), BF),
            dma((3,)),
            dma((2,)),
            dma((2, NCH)),
            dma((2, NCH)),
            dma((2, NCH)),
            dma((2, 2, 3)),
            dma((2, NCH, 3)),
            dma((2, 2, 3)),
            dma((2, NCH, 3)),
            dma((2, 2)),
            dma((2, NCH, 2)),
            dma((2, NCH, 2)),
            dma((2, NCH, 2)),
            dma((2, NCH, 2)),
            dma((2, 2)),
        ],
        compiler_params=pltpu.CompilerParams(
            collective_id=0, has_side_effects=True, vmem_limit_bytes=60 * 2**20
        ),
    )(meta, perm, tokens, grad_out, w_gate[0], w_up[0], w_down[0])
    grad_in, update, second = pl.pallas_call(
        backward_kernel,
        name="combine",
        out_shape=(
            jax.ShapeDtypeStruct((TOK, D), BF),
            jax.ShapeDtypeStruct((Q, D), BF),
            jax.ShapeDtypeStruct((Q, 1), F32),
        ),
        in_specs=[vmem, vmem, vmem, vmem, hbm, hbm, hbm, vmem],
        out_specs=(vmem, vmem, vmem),
        scratch_shapes=[
            pltpu.VMEM((2, ROWS, CW), BF),
            pltpu.VMEM((2, HALF, D), BF),
            pltpu.VMEM((2, 2, ROWS, CW), BF),
            pltpu.VMEM((2, ROWS, D), BF),
            pltpu.VMEM((2, ROWS, CW), BF),
            pltpu.VMEM((ROWS, D), BF),
            pltpu.VMEM((2, ROWS, CW), BF),
            pltpu.VMEM((ROWS, D), BF),
            pltpu.VMEM((2, TOK, CW), BF),
            pltpu.VMEM((2, TOK, CW), BF),
            pltpu.VMEM((TOK, D), BF),
            pltpu.VMEM((2, 2, 4, ROWS, CW), BF),
            pltpu.VMEM((Q, D), F32),
            pltpu.VMEM((Q, 128), F32),
            pltpu.VMEM((D, Q), BF),
            pltpu.VMEM((D, Q), BF),
            dma((2,)),
            dma((2, 2)),
            dma((NCH, 2)),
            dma((2, 2)),
            dma((NCH, 2)),
            dma((2, 3)),
            dma((NCH, 3)),
            dma((2, 3)),
            dma((NCH, 3)),
            dma((2,)),
            dma((NCH,)),
            dma((2, 2)),
        ],
        compiler_params=pltpu.CompilerParams(
            collective_id=1, has_side_effects=True, vmem_limit_bytes=60 * 2**20
        ),
    )(acts, acts_t, sel, perm, rows, w_gate[0], w_up[0], moment_prev.reshape(Q, 1))
    return grad_in, update[None], second.reshape(1, Q)


def solution(mesh):
    placed = (
        P(("dp", "expert"), None),
        P(("dp", "expert"), None),
        P(("dp", "expert"), None),
        P(("dp", "expert"), None),
        P("expert", None, "dp"),
        P("expert", None, "dp"),
        P("expert", "dp", None),
        P("expert", "dp"),
    )
    return jax.shard_map(
        shards,
        mesh=mesh,
        in_specs=placed,
        out_specs=(P(("dp", "expert"), None), P("expert", "dp", None), P("expert", "dp")),
        check_vma=False,
    )
```

time: 766 us -> 345 us (0.45)
  the two profiles are of different devices: /device:TPU:74 before, /device:TPU:0 now
where the time goes in v1:
time: 345 us; the launch traced here: 344 us
  Pallas kernels  332 us (96%)
  local copies, waits for them, and re-layouts  6.39 us (2%)
  other arithmetic  4.31 us (1%)
    pallas_call x1, Pallas kernels, shards(): pl.pallas_call(forward_kernel, name='dispatch', out_shape=(jax.ShapeDtype...  218 us
    pallas_call x1, Pallas kernels, shards(): pl.pallas_call(backward_kernel, name='combine', out_shape=(jax.ShapeDtype...  114 us

profile of v1, /device:TPU:0, one launch (start us, length us, event | category | flops | bytes accessed | tf_op | source)
XLA Modules:
  0.0 343.6 jit_solution(17150842281116963911)
XLA Ops:
  0.6 0.7 convert_bitcast_fusion
  1.3 0.1 pad.2.clone
  1.4 1.3 maximum_maximum_fusion.meta_ref
  2.7 0.7 fusion.perm_ref
  3.4 1.5 copy.11.moment_ref
  4.9 218.4 %dispatch.1 = (bf16[2,4,192,7168]{3,2,1,0:T(8,128)(2,1)}, bf16[2,768,256]{2,1,0:T(8,128)(2,1)}, bf16[3,256,768]{2,1,0:T(8,128)(2,1)}, bf16[192,256]{1,0:T(8,128)(2,1)}) custom-call(f32[8,128]{1,0:T(8,128)} %maximum_maximum_fusion.meta_ref, bf16[192,192]{1,0:T(8,128)(2,1)} %fusion.perm_ref, bf16[128,7168]{1,0:T(8,128)(2,1)} %tok_ref.1, ...), custom_call_target="tpu_custom_call" | custom-call | tf_op jit(solution)/shard_map/dispatch/pallas_call | solution.py:579
  223.4 113.8 %combine.1 = (bf16[128,7168]{1,0:T(8,128)(2,1)}, bf16[256,7168]{1,0:T(8,128)(2,1)}, f32[256,1]{1,0:T(8,128)}) custom-call(bf16[2,768,256]{2,1,0:T(8,128)(2,1)} %get-tuple-element.10.acts, bf16[3,256,768]{2,1,0:T(8,128)(2,1)} %get-tuple-element.11.acts_t, bf16[192,256]{1,0:T(8,128)(2,1)} %get-tuple-element.12.sel_ref, bf16[192,192]{1,0:T(8,128)(2,1)} %fusion.perm_ref, ...), custom_call_target="tpu_custom_call" | custom-call | tf_op jit(solution)/shard_map/combine/pallas_call | solution.py:622
  337.1 1.6 reduce
  338.7 0.0 copy-start
  338.7 3.0 copy.14
  341.7 0.0 copy-done
  341.7 1.8 copy.15
  (2 shorter events, 0.0 us)
Async XLA Ops:
  338.7 3.0 copy-start

commit v2 on v1

v2 whole, which is shorter than its diff:
```python
import functools

import jax
import jax.numpy as jnp
from jax import lax
from jax.experimental import pallas as pl
from jax.experimental.pallas import tpu as pltpu
from jax.sharding import PartitionSpec as P

MESH = pl.DeviceIdType.MESH
BF = jnp.bfloat16
F32 = jnp.float32

moment_decay = 0.95
epsilon = 1e-08

D = 7168
TOK = 128
CAP = 6
Q = 256
ROWS = 192
BLK = 48
SUB = 256

FW = 512
FC = D // FW
F_EARLY = 12
F_LATE = 2 * FC - F_EARLY
BW = 512
BC = D // BW
B_EARLY = 6
B_LATE = BC - B_EARLY

ACROSS = ((0, 0, 0, 1),) + tuple((0, d, 0, 0) for d in (1, 2, 3)) + tuple((0, 0, d, 0) for d in (1, 2, 3))
COLUMN = ((1, 0, 0, 0), (3, 0, 0, 0), (2, 0, 0, 0), (1, 0, 0, 1), (3, 0, 0, 1), (2, 0, 0, 1))
PLUS_MINUS = (1, 3)


def place():
    y = lax.axis_index("dp")
    e = lax.axis_index("expert")
    return y, e // 8, (e // 2) % 4, e % 2


def peer(here, dy, dz, dx, dc):
    y, z, x, c = here
    expert = (((z + dz) % 4) * 4 + (x + dx) % 4) * 2 + (c + dc) % 2
    return {"dp": (y + dy) % 4, "expert": expert}


def remote(src, dst, send, recv, device):
    return pltpu.make_async_remote_copy(
        src_ref=src,
        dst_ref=dst,
        send_sem=send,
        recv_sem=recv,
        device_id=device,
        device_id_type=MESH,
    )


def greet(here, partners):
    barrier = pltpu.get_barrier_semaphore()
    for offset in partners:
        pl.semaphore_signal(barrier, inc=1, device_id=peer(here, *offset), device_id_type=MESH)
    pl.semaphore_wait(barrier, len(partners))


def at(index, size, align):
    return pl.ds(pl.multiple_of(index * size, align), size)


def nt(a, b):
    return lax.dot_general(a, b, (((1,), (1,)), ((), ())), preferred_element_type=F32)


def tn(a, b):
    return lax.dot_general(a, b, (((0,), (0,)), ((), ())), preferred_element_type=F32)


def nn(a, b):
    return jnp.dot(a, b, preferred_element_type=F32)


def tiles(width):
    return [slice(j, j + SUB) for j in range(0, width, SUB)]


def swap_matrix():
    out = lax.broadcasted_iota(jnp.int32, (ROWS, ROWS), 0)
    row = lax.broadcasted_iota(jnp.int32, (ROWS, ROWS), 1)

    def steps(value, size):
        return sum((value >= size * n).astype(jnp.int32) for n in (1, 2, 3))

    outer = steps(out, 48)
    inner = steps(out - 48 * outer, 12)
    return (row - out == 36 * (inner - outer)).astype(F32).astype(BF)


def when(k, count, body):
    pl.when((k >= 0) & (k < count))(lambda: body(k))


def forward_kernel(
    routes_ref,
    prob_ref,
    tok_ref,
    cot_ref,
    wg_hbm,
    wu_hbm,
    wd_hbm,
    rows,
    acts,
    acts_t,
    sel,
    metas,
    gp,
    perm,
    raw,
    zs,
    za,
    xs,
    raw4,
    zs4,
    za4,
    xs4,
    stage,
    stage4,
    acc,
    wg,
    wu,
    wd,
    w_sem,
    m_s,
    m_r,
    raw_l,
    raw_s,
    raw_r,
    z_s,
    z_r,
    x_s,
    x_r,
    x_l,
    y_s,
    y_r,
    f_s,
    f_r,
    st_l,
    own_l,
    own_s,
    own_r,
    yy_s,
    yy_r,
    ff_s,
    ff_r,
    cc_s,
    cc_r,
    zz_s,
    zz_r,
    xx_s,
    xx_r,
    xx_l,
    st4_l,
):
    here = place()
    y, z, x, c = here
    sources = (tok_ref, cot_ref)
    mine = at(c, TOK, TOK)

    def cols(k):
        return at(k, FW, 128)

    greet(here, ACROSS + COLUMN)

    first = lax.broadcasted_iota(jnp.int32, (8, TOK), 0) == 0
    metas[y, c] = jnp.where(first, routes_ref[...].astype(F32), prob_ref[...])
    others = COLUMN + ((0, 0, 0, 1),)

    def meta_copy(i):
        return remote(
            metas.at[y, c], metas.at[y, c], m_s.at[i], m_r.at[i], peer(here, *others[i])
        )

    for i in range(len(others)):
        meta_copy(i).start()

    def yy_copy(k, i):
        return remote(
            cot_ref.at[:, cols(k)],
            raw4.at[k, y, mine, :],
            yy_s.at[k, i],
            yy_r.at[k, i],
            peer(here, PLUS_MINUS[i], 0, 0, 0),
        )

    def ff_copy(k, i):
        src = (y + PLUS_MINUS[1 - i]) % 4
        half = raw4.at[k, src, pl.ds(pl.multiple_of(c * TOK + i * 64, 64), 64), :]
        return remote(
            half, half, ff_s.at[k, i], ff_r.at[k, i], peer(here, PLUS_MINUS[i], 0, 0, 0)
        )

    def cc_copy(k, i):
        block = raw4.at[k, (y + (3, 1, 2)[i]) % 4, mine, :]
        return remote(block, block, cc_s.at[k, i], cc_r.at[k, i], peer(here, 0, 0, 0, 1))

    def own_local(k):
        return pltpu.make_async_copy(
            cot_ref.at[:, cols(k)], raw4.at[k, y, mine, :], own_l.at[k]
        )

    def own_remote(k):
        return remote(
            cot_ref.at[:, cols(k)],
            raw4.at[k, y, mine, :],
            own_s.at[k],
            own_r.at[k],
            peer(here, 0, 0, 0, 1),
        )

    def zz_copy(k, d):
        return remote(
            zs4.at[k % 2, :, at((z + d) % 4, BLK, 16), :],
            za4.at[k, :, at(z, BLK, 16), :],
            zz_s.at[k % 2, d - 1],
            zz_r.at[k, d - 1],
            peer(here, 0, d, 0, 0),
        )

    def xx_copy(k, d):
        return remote(
            xs4.at[k % 2, :, at((x + d) % 4, BLK, 16), :],
            rows.at[1, :, at(x, BLK, 16), cols(k)],
            xx_s.at[k % 2, d - 1],
            xx_r.at[k, d - 1],
            peer(here, 0, 0, d, 0),
        )

    def xx_own(k):
        return pltpu.make_async_copy(
            xs4.at[k % 2, :, at(x, BLK, 16), :],
            rows.at[1, :, at(x, BLK, 16), cols(k)],
            xx_l.at[k % 2],
        )

    def stage4_copy(k):
        return pltpu.make_async_copy(
            rows.at[1, :, :, cols(k)], stage4.at[k % 2], st4_l.at[k % 2]
        )

    def early_send(k):
        for i in range(2):
            yy_copy(k, i).start()

    def early_pass(k):
        for i in range(2):
            yy_copy(k, i).wait_recv()
            ff_copy(k, i).start()
            cc_copy(k, i).start()

    def early_rest(k):
        for i in range(2):
            ff_copy(k, i).wait_recv()
        cc_copy(k, 2).start()

    def early_select(k):
        own_local(k).wait()
        own_remote(k).wait()
        for i in range(3):
            cc_copy(k, i).wait_recv()

        def block(b, carry):
            for out in tiles(FW):
                picked = nn(sel[b], raw4[k, b, :, out]) * gp[b, :, 0:1]
                zs4[k % 2, b, :, out] = picked.astype(BF)
            za4[k, b, at(z, BLK, 16), :] = zs4[k % 2, b, at(z, BLK, 16), :]
            return carry

        lax.fori_loop(0, 4, block, 0)
        for d in (2, 1, 3):
            zz_copy(k, d).start()

    def early_turn(k):
        for d in (1, 2, 3):
            zz_copy(k, d).wait_recv()

        def block(b, carry):
            for out in tiles(FW):
                xs4[k % 2, b, :, out] = nn(perm[...], za4[k, b, :, out]).astype(BF)
            return carry

        lax.fori_loop(0, 4, block, 0)
        for d in (2, 1, 3):
            xx_copy(k, d).start()
        xx_own(k).start()

    def early_fetch(k):
        for d in (1, 2, 3):
            xx_copy(k, d).wait_recv()
        xx_own(k).wait()
        stage4_copy(k).start()

    def early_accumulate(k):
        stage4_copy(k).wait()

        def block(b, carry):
            acc[2, at(b, ROWS, 16), :] += nt(stage4[k % 2, b], wd[:, cols(k)])
            return carry

        lax.fori_loop(0, 4, block, 0)

    def which(i):
        a = i // FC
        return a, cols(i - a * (FC - F_EARLY))

    def raw_copies(i):
        a = i // FC
        src = sources[a].at[:, cols(i - a * (FC - F_EARLY))]
        dst = raw.at[i, mine, :]
        return (
            pltpu.make_async_copy(src, dst, raw_l.at[i]),
            remote(src, dst, raw_s.at[i], raw_r.at[i], peer(here, 0, 0, 0, 1)),
        )

    def raw_waits(i):
        src = tok_ref.at[:, cols(0)]
        dst = raw.at[i, mine, :]
        return (
            pltpu.make_async_copy(src, dst, raw_l.at[i]),
            remote(src, dst, raw_s.at[i], raw_r.at[i], peer(here, 0, 0, 0, 1)),
        )

    def z_copy(i, d):
        return remote(
            zs.at[i % 2, at((z + d) % 4, BLK, 16), :],
            za.at[i, at(z, BLK, 16), :],
            z_s.at[i % 2, d - 1],
            z_r.at[i, d - 1],
            peer(here, 0, d, 0, 0),
        )

    def x_copy(i, d):
        a, span = which(i)
        return remote(
            xs.at[i % 2, at((x + d) % 4, BLK, 16), :],
            rows.at[a, y, at(x, BLK, 16), span],
            x_s.at[i % 2, d - 1],
            x_r.at[i, d - 1],
            peer(here, 0, 0, d, 0),
        )

    def x_own(i):
        a, span = which(i)
        return pltpu.make_async_copy(
            xs.at[i % 2, at(x, BLK, 16), :], rows.at[a, y, at(x, BLK, 16), span], x_l.at[i % 2]
        )

    def y_copy(i, p):
        a, span = which(i)
        block = rows.at[a, y, :, span]
        return remote(
            block, block, y_s.at[i, p], y_r.at[i, p], peer(here, PLUS_MINUS[p], 0, 0, 0)
        )

    def f_copy(i, p):
        a, span = which(i)
        half = rows.at[a, (y + PLUS_MINUS[1 - p]) % 4, pl.ds(p * 96, 96), span]
        return remote(half, half, f_s.at[i, p], f_r.at[i, p], peer(here, PLUS_MINUS[p], 0, 0, 0))

    def stage_copy(i):
        a, span = which(i)
        return pltpu.make_async_copy(rows.at[a, :, :, span], stage.at[i % 2], st_l.at[i % 2])

    def late_select(i):
        for copy in raw_waits(i):
            copy.wait()
        scale = jnp.where(i // FC == 1, gp[y], 1.0)[:, 0:1]
        for out in tiles(FW):
            zs[i % 2, :, out] = (nn(sel[y], raw[i, :, out]) * scale).astype(BF)
        for d in (2, 1, 3):
            z_copy(i, d).start()
        za[i, at(z, BLK, 16), :] = zs[i % 2, at(z, BLK, 16), :]

    def late_turn(i):
        for d in (1, 2, 3):
            z_copy(i, d).wait_recv()
        for out in tiles(FW):
            xs[i % 2, :, out] = nn(perm[...], za[i, :, out]).astype(BF)
        for d in (2, 1, 3):
            x_copy(i, d).start()
        x_own(i).start()

    def late_spread(i):
        for d in (1, 2, 3):
            x_copy(i, d).wait_recv()
        x_own(i).wait()
        for p in range(2):
            y_copy(i, p).start()

    def late_pass(i):
        for p in range(2):
            y_copy(i, p).wait_recv()
            f_copy(i, p).start()

    def late_fetch(i):
        for p in range(2):
            f_copy(i, p).wait_recv()
        stage_copy(i).start()

    def late_accumulate(i):
        stage_copy(i).wait()
        a, span = which(i)

        @pl.when(a == 0)
        def _():
            def block(b, carry):
                block_rows = at(b, ROWS, 16)
                tokens = stage[i % 2, b]
                acc[0, block_rows, :] += nn(tokens, wg[span, :])
                acc[1, block_rows, :] += nn(tokens, wu[span, :])
                return carry

            lax.fori_loop(0, 4, block, 0)

        @pl.when(a == 1)
        def _():
            def block(b, carry):
                acc[2, at(b, ROWS, 16), :] += nt(stage[i % 2, b], wd[:, span])
                return carry

            lax.fori_loop(0, 4, block, 0)

    def drain(copy, count, base):
        def body(k):
            for i in range(count):
                copy(k, base + i).wait_send()

        return body

    early_send(0)
    for i in range(F_LATE):
        for copy in raw_copies(i):
            copy.start()
        if i < F_EARLY:
            own_local(i).start()
            own_remote(i).start()
    weights = [
        pltpu.make_async_copy(src, dst, w_sem.at[i])
        for i, (src, dst) in enumerate(((wg_hbm, wg), (wu_hbm, wu), (wd_hbm, wd)))
    ]
    for copy in weights:
        copy.start()
    perm[...] = swap_matrix()
    acc[...] = jnp.zeros_like(acc)
    for i in range(len(others)):
        meta_copy(i).wait()

    def plan(b, carry):
        earlier = (
            (
                lax.broadcasted_iota(jnp.int32, (TOK, TOK), 0)
                < lax.broadcasted_iota(jnp.int32, (TOK, TOK), 1)
            )
            .astype(F32)
            .astype(BF)
        )
        weight = jnp.zeros((ROWS, 1), F32)
        for m in range(2):
            route = metas[b, m, 0:1, :].astype(jnp.int32)
            prob = metas[b, m, 1:2, :]
            onehot = (lax.broadcasted_iota(jnp.int32, (32, TOK), 0) == route).astype(F32)
            before = nn(onehot.astype(BF), earlier)
            slot = jnp.sum(onehot * before, axis=0, keepdims=True).astype(jnp.int32)
            row = ((route >> 1) * 2 + m) * CAP + slot
            row = jnp.where((route & 1) == c, row, -1)
            chosen = lax.broadcasted_iota(jnp.int32, (ROWS, TOK), 0) == row
            sel[b, :, m * TOK : (m + 1) * TOK] = chosen.astype(F32).astype(BF)
            weight = weight + jnp.sum(jnp.where(chosen, prob, 0.0), axis=1, keepdims=True)
        gp[b] = jnp.broadcast_to(weight, (ROWS, 128))
        return carry

    lax.fori_loop(0, 4, plan, 0)

    def step(t, carry):
        when(t - 2, F_LATE, drain(z_copy, 3, 1))
        when(t - 3, F_LATE, drain(x_copy, 3, 1))
        when(t - 4, F_LATE, drain(y_copy, 2, 0))
        when(t - 5, F_LATE, drain(f_copy, 2, 0))
        when(t - 1, F_EARLY, drain(yy_copy, 2, 0))
        when(t - 2, F_EARLY, drain(ff_copy, 2, 0))
        when(t - 3, F_EARLY, drain(cc_copy, 3, 0))
        when(t - 4, F_EARLY, drain(zz_copy, 3, 1))
        when(t - 5, F_EARLY, drain(xx_copy, 3, 1))

        when(t, F_LATE, late_select)
        when(t + 1, F_EARLY, early_send)
        when(t, F_EARLY, early_pass)
        when(t - 1, F_LATE, late_turn)
        when(t - 1, F_EARLY, early_rest)
        when(t - 2, F_LATE, late_spread)
        when(t - 2, F_EARLY, early_select)
        when(t - 3, F_LATE, late_pass)
        when(t - 3, F_EARLY, early_turn)
        when(t - 4, F_LATE, late_fetch)
        when(t - 4, F_EARLY, early_fetch)

        @pl.when(t == 5)
        def _():
            for copy in weights:
                copy.wait()

        when(t - 5, F_LATE, late_accumulate)
        when(t - 5, F_EARLY, early_accumulate)
        return carry

    lax.fori_loop(0, F_LATE + 5, step, 0)

    def finish(b, carry):
        part = at(b, Q, 256)
        gate, up, grad = acc[0, part, :], acc[1, part, :], acc[2, part, :]
        sig = jax.nn.sigmoid(gate)
        silu = gate * sig
        hidden = silu * up
        gate_grad = grad * up * sig * (1.0 + gate * (1.0 - sig))
        up_grad = grad * silu
        acts[0, part, :] = gate_grad.astype(BF)
        acts[1, part, :] = up_grad.astype(BF)
        acts_t[0, :, part] = hidden.T.astype(BF)
        acts_t[1, :, part] = gate_grad.T.astype(BF)
        acts_t[2, :, part] = up_grad.T.astype(BF)
        return carry

    lax.fori_loop(0, 3, finish, 0)


def backward_kernel(
    acts,
    acts_t,
    sel,
    rows,
    wg_hbm,
    wu_hbm,
    moment_ref,
    grad_ref,
    update_ref,
    second_ref,
    perm,
    far,
    relay,
    near,
    summed,
    xs,
    xa,
    zs,
    za,
    cs,
    co,
    cr,
    xs4,
    xa4,
    zs4,
    za4,
    cs4,
    co4,
    cr4,
    relay4,
    summed4,
    stage,
    dw,
    squares,
    wg,
    wu,
    w_sem,
    p_s,
    p_r,
    n_s,
    n_r,
    x_s,
    x_r,
    z_s,
    z_r,
    c_s,
    c_r,
    xx_s,
    xx_r,
    zz_s,
    zz_r,
    cc_s,
    cc_r,
    pp_s,
    pp_r,
    nn_s,
    nn_r,
    st_l,
):
    here = place()
    y, z, x, c = here

    def cols(k):
        return at(k, BW, 128)

    def tile(k, out):
        return pl.ds(pl.multiple_of(k * BW + out.start, 128), SUB)

    greet(here, ACROSS + COLUMN[:2])
    weights = [
        pltpu.make_async_copy(src, dst, w_sem.at[i])
        for i, (src, dst) in enumerate(((wg_hbm, wg), (wu_hbm, wu)))
    ]
    for copy in weights:
        copy.start()

    def stage_copy(a, k):
        return pltpu.make_async_copy(
            rows.at[a, :, :, cols(k)], stage.at[a, k % 2], st_l.at[a, k % 2]
        )

    for a in range(2):
        stage_copy(a, 0).start()
    squares[...] = jnp.zeros_like(squares)
    perm[...] = swap_matrix()
    for copy in weights:
        copy.wait()

    def partial(block, k, out):
        block_rows = at(block, ROWS, 16)
        total = nt(acts[0, block_rows, :], wg[tile(k, out), :])
        total = total + nt(acts[1, block_rows, :], wu[tile(k, out), :])
        return total.astype(BF)

    def p_copy(k, i):
        return remote(
            far.at[k % 2, pl.ds(i * 96, 96), :],
            relay.at[k, i],
            p_s.at[k % 2, i],
            p_r.at[k, i],
            peer(here, PLUS_MINUS[i], 0, 0, 0),
        )

    def n_copy(k, i):
        return remote(
            near.at[i, k % 2],
            summed.at[k, i],
            n_s.at[k % 2, i],
            n_r.at[k, i],
            peer(here, PLUS_MINUS[i], 0, 0, 0),
        )

    def x_copy(k, d):
        return remote(
            xs.at[k % 2, at((x + d) % 4, BLK, 16), :],
            xa.at[k, at(x, BLK, 16), :],
            x_s.at[k % 2, d - 1],
            x_r.at[k, d - 1],
            peer(here, 0, 0, d, 0),
        )

    def z_copy(k, d):
        return remote(
            zs.at[k % 2, at((z + d) % 4, BLK, 16), :],
            za.at[k, at(z, BLK, 16), :],
            z_s.at[k % 2, d - 1],
            z_r.at[k, d - 1],
            peer(here, 0, d, 0, 0),
        )

    def c_copy(k):
        return remote(cs.at[k % 2], cr.at[k], c_s.at[k % 2], c_r.at[k], peer(here, 0, 0, 0, 1))

    def late_far(k):
        for out in tiles(BW):
            far[k % 2, :, out] = partial((y + 2) % 4, k, out)
        for i in range(2):
            p_copy(k, i).start()

    def late_near(k):
        for i in range(2):
            p_copy(k, i).wait_recv()
            added, plain = slice(i * 96, i * 96 + 96), slice(96 - i * 96, 192 - i * 96)
            for out in tiles(BW):
                term = partial((y + PLUS_MINUS[i]) % 4, k, out)
                both = term[added].astype(F32) + relay[k, i, :, out].astype(F32)
                near[i, k % 2, added, out] = both.astype(BF)
                near[i, k % 2, plain, out] = term[plain]
            n_copy(k, i).start()

    def late_total(k):
        for i in range(2):
            n_copy(k, i).wait_recv()
        for out in tiles(BW):
            whole = partial(y, k, out).astype(F32)
            whole = whole + summed[k, 0, :, out].astype(F32)
            whole = whole + summed[k, 1, :, out].astype(F32)
            xs[k % 2, :, out] = whole.astype(BF)
        for d in (2, 1, 3):
            x_copy(k, d).start()
        xa[k, at(x, BLK, 16), :] = xs[k % 2, at(x, BLK, 16), :]

    def late_turn(k):
        for d in (1, 2, 3):
            x_copy(k, d).wait_recv()
        for out in tiles(BW):
            zs[k % 2, :, out] = nn(perm[...], xa[k, :, out]).astype(BF)
        for d in (2, 1, 3):
            z_copy(k, d).start()
        za[k, at(z, BLK, 16), :] = zs[k % 2, at(z, BLK, 16), :]

    def late_unselect(k):
        for d in (1, 2, 3):
            z_copy(k, d).wait_recv()
        for out in tiles(BW):
            block = za[k, :, out]
            cs[k % 2, :, out] = tn(sel[y, :, at(1 - c, TOK, TOK)], block).astype(BF)
            co[k % 2, :, out] = tn(sel[y, :, at(c, TOK, TOK)], block).astype(BF)
        c_copy(k).start()

    def late_join(k):
        c_copy(k).wait()
        whole = co[k % 2].astype(F32) + cr[k].astype(F32)
        grad_ref[:, cols(k)] = whole.astype(BF)

    def xx_copy(k, d):
        return remote(
            xs4.at[k % 2, :, at((x + d) % 4, BLK, 16), :],
            xa4.at[k, :, at(x, BLK, 16), :],
            xx_s.at[k % 2, d - 1],
            xx_r.at[k, d - 1],
            peer(here, 0, 0, d, 0),
        )

    def zz_copy(k, d):
        return remote(
            zs4.at[k % 2, :, at((z + d) % 4, BLK, 16), :],
            za4.at[k, :, at(z, BLK, 16), :],
            zz_s.at[k % 2, d - 1],
            zz_r.at[k, d - 1],
            peer(here, 0, d, 0, 0),
        )

    def cc_copy(k):
        return remote(
            cs4.at[k % 2], cr4.at[k], cc_s.at[k % 2], cc_r.at[k], peer(here, 0, 0, 0, 1)
        )

    def pp_copy(k, i):
        return remote(
            cr4.at[k, (y + 2) % 4, pl.ds(i * 64, 64), :],
            relay4.at[k, i],
            pp_s.at[k, i],
            pp_r.at[k, i],
            peer(here, PLUS_MINUS[i], 0, 0, 0),
        )

    def nn_copy(k, i):
        return remote(
            cr4.at[k, (y + PLUS_MINUS[i]) % 4],
            summed4.at[k, i],
            nn_s.at[k, i],
            nn_r.at[k, i],
            peer(here, PLUS_MINUS[i], 0, 0, 0),
        )

    def early_terms(k):
        def block(b, carry):
            for out in tiles(BW):
                xs4[k % 2, b, :, out] = partial(b, k + B_LATE, out)
            xa4[k, b, at(x, BLK, 16), :] = xs4[k % 2, b, at(x, BLK, 16), :]
            return carry

        lax.fori_loop(0, 4, block, 0)
        for d in (2, 1, 3):
            xx_copy(k, d).start()

    def early_turn(k):
        for d in (1, 2, 3):
            xx_copy(k, d).wait_recv()

        def block(b, carry):
            for out in tiles(BW):
                zs4[k % 2, b, :, out] = nn(perm[...], xa4[k, b, :, out]).astype(BF)
            za4[k, b, at(z, BLK, 16), :] = zs4[k % 2, b, at(z, BLK, 16), :]
            return carry

        lax.fori_loop(0, 4, block, 0)
        for d in (2, 1, 3):
            zz_copy(k, d).start()

    def early_unselect(k):
        for d in (1, 2, 3):
            zz_copy(k, d).wait_recv()

        def block(b, carry):
            for out in tiles(BW):
                whole = za4[k, b, :, out]
                cs4[k % 2, b, :, out] = tn(sel[b, :, at(1 - c, TOK, TOK)], whole).astype(BF)
                co4[k % 2, b, :, out] = tn(sel[b, :, at(c, TOK, TOK)], whole).astype(BF)
            return carry

        lax.fori_loop(0, 4, block, 0)
        cc_copy(k).start()

    def early_far(k):
        cc_copy(k).wait()

        def block(b, carry):
            whole = co4[k % 2, b].astype(F32) + cr4[k, b].astype(F32)
            cr4[k, b] = whole.astype(BF)
            return carry

        lax.fori_loop(0, 4, block, 0)
        for i in range(2):
            pp_copy(k, i).start()

    def early_near(k):
        for i in range(2):
            pp_copy(k, i).wait_recv()
            block, added = (y + PLUS_MINUS[i]) % 4, slice(i * 64, i * 64 + 64)
            both = cr4[k, block, added, :].astype(F32) + relay4[k, i].astype(F32)
            cr4[k, block, added, :] = both.astype(BF)
            nn_copy(k, i).start()

    def early_join(k):
        whole = cr4[k, y].astype(F32)
        for i in range(2):
            nn_copy(k, i).wait()
            whole = whole + summed4[k, i].astype(F32)
        grad_ref[:, cols(k + B_LATE)] = whole.astype(BF)

    def weight_grads(k):
        for a in range(2):
            stage_copy(a, k).wait()

        @pl.when(k + 1 < BC)
        def _():
            for a in range(2):
                stage_copy(a, k + 1).start()

        for out in tiles(BW):
            cot_rows = stage[1, k % 2, :, :, out].reshape(4 * ROWS, SUB)
            tok_rows = stage[0, k % 2, :, :, out].reshape(4 * ROWS, SUB)
            down = nn(acts_t[0], cot_rows)
            dw[:, tile(k, out)] = down
            gate = nn(acts_t[1], tok_rows)
            up = nn(acts_t[2], tok_rows)
            sq = down * down + gate * gate + up * up
            squares[...] += sq[:, 0:128] + sq[:, 128:256]

    def update(k):
        @pl.when(k == 0)
        def _():
            mean = jnp.sum(squares[...], axis=1, keepdims=True) / (3.0 * D)
            old = jnp.broadcast_to(moment_ref[...], (128, Q)).T
            second = moment_decay * old + (1.0 - moment_decay) * mean
            second_ref[...] = second.T[0:1, :]
            squares[...] = 1.0 / (jnp.sqrt(second) + epsilon)

        for j in range(BW // 128):
            out = pl.ds(pl.multiple_of(k * BW + j * 128, 128), 128)
            update_ref[:, out] = (dw[:, out] * squares[...]).astype(BF)

    def drain(copy, count, base):
        def body(k):
            for i in range(count):
                copy(k, base + i).wait_send()

        return body

    def step(t, carry):
        when(t - 2, B_LATE, drain(p_copy, 2, 0))
        when(t - 3, B_LATE, drain(n_copy, 2, 0))
        when(t - 4, B_LATE, drain(x_copy, 3, 1))
        when(t - 5, B_LATE, drain(z_copy, 3, 1))
        when(t - 2, B_EARLY, drain(xx_copy, 3, 1))
        when(t - 3, B_EARLY, drain(zz_copy, 3, 1))
        when(t - 5, B_EARLY, drain(pp_copy, 2, 0))

        when(t, B_LATE, late_far)
        when(t, B_EARLY, early_terms)
        when(t - 1, B_LATE, late_near)
        when(t - 1, B_EARLY, early_turn)
        when(t - 2, B_LATE, late_total)
        when(t - 2, B_EARLY, early_unselect)
        when(t - 3, B_LATE, late_turn)
        when(t - 3, B_EARLY, early_far)
        when(t - 4, B_LATE, late_unselect)
        when(t - 4, B_EARLY, early_near)
        when(t - 5, B_LATE, late_join)
        when(t - 5, B_EARLY, early_join)
        for n in range(2):
            when(t * 2 + n, BC, weight_grads)
        for n in range(3):
            when((t - BC // 2) * 3 + n, BC, update)
        return carry

    lax.fori_loop(0, B_LATE + 5, step, 0)


def shards(tokens, grad_out, routes, gate_prob, w_gate, w_up, w_down, moment_prev):
    vmem = pl.BlockSpec(memory_space=pltpu.VMEM)
    hbm = pl.BlockSpec(memory_space=pltpu.HBM)
    dma = pltpu.SemaphoreType.DMA

    def held(*shape):
        return pltpu.VMEM(shape, BF)

    rows, acts, acts_t, sel = pl.pallas_call(
        forward_kernel,
        name="dispatch",
        out_shape=(
            jax.ShapeDtypeStruct((2, 4, ROWS, D), BF),
            jax.ShapeDtypeStruct((2, 4 * ROWS, Q), BF),
            jax.ShapeDtypeStruct((3, Q, 4 * ROWS), BF),
            jax.ShapeDtypeStruct((4, ROWS, 2 * TOK), BF),
        ),
        in_specs=[vmem, vmem, hbm, hbm, hbm, hbm, hbm],
        out_specs=(hbm, vmem, vmem, vmem),
        scratch_shapes=[
            pltpu.VMEM((4, 2, 8, TOK), F32),
            pltpu.VMEM((4, ROWS, 128), F32),
            held(ROWS, ROWS),
            held(F_LATE, 2 * TOK, FW),
            held(2, ROWS, FW),
            held(F_LATE, ROWS, FW),
            held(2, ROWS, FW),
            held(F_EARLY, 4, 2 * TOK, FW),
            held(2, 4, ROWS, FW),
            held(F_EARLY, 4, ROWS, FW),
            held(2, 4, ROWS, FW),
            held(2, 4, ROWS, FW),
            held(2, 4, ROWS, FW),
            pltpu.VMEM((3, 4 * ROWS, Q), F32),
            held(D, Q),
            held(D, Q),
            held(Q, D),
            dma((3,)),
            dma((7,)),
            dma((7,)),
            dma((F_LATE,)),
            dma((F_LATE,)),
            dma((F_LATE,)),
            dma((2, 3)),
            dma((F_LATE, 3)),
            dma((2, 3)),
            dma((F_LATE, 3)),
            dma((2,)),
            dma((F_LATE, 2)),
            dma((F_LATE, 2)),
            dma((F_LATE, 2)),
            dma((F_LATE, 2)),
            dma((2,)),
            dma((F_EARLY,)),
            dma((F_EARLY,)),
            dma((F_EARLY,)),
            dma((F_EARLY, 2)),
            dma((F_EARLY, 2)),
            dma((F_EARLY, 2)),
            dma((F_EARLY, 2)),
            dma((F_EARLY, 3)),
            dma((F_EARLY, 3)),
            dma((2, 3)),
            dma((F_EARLY, 3)),
            dma((2, 3)),
            dma((F_EARLY, 3)),
            dma((2,)),
            dma((2,)),
        ],
        compiler_params=pltpu.CompilerParams(
            collective_id=0, has_side_effects=True, vmem_limit_bytes=60 * 2**20
        ),
    )(
        routes.reshape(1, TOK),
        gate_prob.reshape(1, TOK),
        tokens,
        grad_out,
        w_gate[0],
        w_up[0],
        w_down[0],
    )
    grad_in, update, second = pl.pallas_call(
        backward_kernel,
        name="combine",
        out_shape=(
            jax.ShapeDtypeStruct((TOK, D), BF),
            jax.ShapeDtypeStruct((Q, D), BF),
            jax.ShapeDtypeStruct((1, Q), F32),
        ),
        in_specs=[vmem, vmem, vmem, hbm, hbm, hbm, vmem],
        out_specs=(vmem, vmem, vmem),
        scratch_shapes=[
            held(ROWS, ROWS),
            held(2, ROWS, BW),
            held(B_LATE, 2, 96, BW),
            held(2, 2, ROWS, BW),
            held(B_LATE, 2, ROWS, BW),
            held(2, ROWS, BW),
            held(B_LATE, ROWS, BW),
            held(2, ROWS, BW),
            held(B_LATE, ROWS, BW),
            held(2, TOK, BW),
            held(2, TOK, BW),
            held(B_LATE, TOK, BW),
            held(2, 4, ROWS, BW),
            held(B_EARLY, 4, ROWS, BW),
            held(2, 4, ROWS, BW),
            held(B_EARLY, 4, ROWS, BW),
            held(2, 4, TOK, BW),
            held(2, 4, TOK, BW),
            held(B_EARLY, 4, TOK, BW),
            held(B_EARLY, 2, 64, BW),
            held(B_EARLY, 2, TOK, BW),
            held(2, 2, 4, ROWS, BW),
            pltpu.VMEM((Q, D), F32),
            pltpu.VMEM((Q, 128), F32),
            held(D, Q),
            held(D, Q),
            dma((2,)),
            dma((2, 2)),
            dma((B_LATE, 2)),
            dma((2, 2)),
            dma((B_LATE, 2)),
            dma((2, 3)),
            dma((B_LATE, 3)),
            dma((2, 3)),
            dma((B_LATE, 3)),
            dma((2,)),
            dma((B_LATE,)),
            dma((2, 3)),
            dma((B_EARLY, 3)),
            dma((2, 3)),
            dma((B_EARLY, 3)),
            dma((2,)),
            dma((B_EARLY,)),
            dma((B_EARLY, 2)),
            dma((B_EARLY, 2)),
            dma((B_EARLY, 2)),
            dma((B_EARLY, 2)),
            dma((2, 2)),
        ],
        compiler_params=pltpu.CompilerParams(
            collective_id=1, has_side_effects=True, vmem_limit_bytes=60 * 2**20
        ),
    )(acts, acts_t, sel, rows, w_gate[0], w_up[0], moment_prev)
    return grad_in, update[None], second


def solution(mesh):
    placed = (
        P(("dp", "expert"), None),
        P(("dp", "expert"), None),
        P(("dp", "expert"), None),
        P(("dp", "expert"), None),
        P("expert", None, "dp"),
        P("expert", None, "dp"),
        P("expert", "dp", None),
        P("expert", "dp"),
    )
    return jax.shard_map(
        shards,
        mesh=mesh,
        in_specs=placed,
        out_specs=(P(("dp", "expert"), None), P("expert", "dp", None), P("expert", "dp")),
        check_vma=False,
    )
```

time: 345 us -> 312 us (0.904)
  Pallas kernels: 332 us -> 304 us
  other arithmetic: 4.31 us -> 0 us
    pallas_call x1, Pallas kernels: 218 us -> 193 us  [shards(): pl.pallas_call(forward_kernel, name='dispatch', out_shape=(jax.ShapeDtype...]
where the time goes in v2:
time: 312 us; the launch traced here: 310 us
  Pallas kernels  304 us (97%)
  local copies, waits for them, and re-layouts  5.4 us (2%)
    pallas_call x1, Pallas kernels, shards(): pl.pallas_call(forward_kernel, name='dispatch', out_shape=(jax.ShapeDtype...  193 us
    pallas_call x1, Pallas kernels, shards(): pl.pallas_call(backward_kernel, name='combine', out_shape=(jax.ShapeDtype...  111 us

profile of v2, /device:TPU:0, one launch (start us, length us, event | category | flops | bytes accessed | tf_op | source)
XLA Modules:
  0.0 310.0 jit_solution(12257451386776837830)
XLA Ops:
  0.6 193.4 %dispatch.1 = (bf16[2,4,192,7168]{3,2,1,0:T(8,128)(2,1)}, bf16[2,768,256]{2,1,0:T(8,128)(2,1)}, bf16[3,256,768]{2,1,0:T(8,128)(2,1)}, bf16[4,192,256]{2,1,0:T(8,128)(2,1)}) custom-call(s32[1,128]{1,0:T(1,128)} %bitcast.12, f32[1,128]{1,0:T(1,128)} %bitcast.13, bf16[128,7168]{1,0:T(8,128)(2,1)} %tok_ref.1, bf16[128,7168]{1,0:T(8,128)(2,1)} %cot_ref.1, ...), custom_call_target="tpu_custom_call" | custom-call | tf_op jit(solution)/shard_map/dispatch/pallas_call | solution.py:907
  194.0 110.6 %combine.1 = (bf16[128,7168]{1,0:T(8,128)(2,1)}, bf16[256,7168]{1,0:T(8,128)(2,1)}, f32[1,256]{1,0:T(1,128)}) custom-call(bf16[2,768,256]{2,1,0:T(8,128)(2,1)} %get-tuple-element.10.acts, bf16[3,256,768]{2,1,0:T(8,128)(2,1)} %get-tuple-element.11.acts_t, bf16[4,192,256]{2,1,0:T(8,128)(2,1)} %get-tuple-element.12.sel, ...), custom_call_target="tpu_custom_call" | custom-call | tf_op jit(solution)/shard_map/combine/pallas_call | solution.py:980
  304.6 0.0 copy-start
  304.6 3.0 copy.14
  307.6 0.0 copy-done
  307.6 0.0 copy-start.1
  307.6 1.8 copy.15
  309.4 0.0 copy-done.1
  309.4 0.6 copy.16
Async XLA Ops:
  304.6 3.0 copy-start
  307.6 1.8 copy-start.1

commit v3 on v2

--- a/solution.py
+++ b/solution.py
@@ -24,12 +24,16 @@
 
 FW = 512
 FC = D // FW
-F_EARLY = 12
-F_LATE = 2 * FC - F_EARLY
+EW = 384
+F_EARLY = 16
+F_DONE = F_EARLY * EW // FW
+F_LATE = 2 * FC - F_DONE
 BW = 512
 BC = D // BW
-B_EARLY = 6
-B_LATE = BC - B_EARLY
+CW = 384
+B_EARLY = 8
+B_LATE = (D - B_EARLY * CW) // BW
+B_FROM = B_LATE * BW
 
 ACROSS = ((0, 0, 0, 1),) + tuple((0, d, 0, 0) for d in (1, 2, 3)) + tuple((0, 0, d, 0) for d in (1, 2, 3))
 COLUMN = ((1, 0, 0, 0), (3, 0, 0, 0), (2, 0, 0, 0), (1, 0, 0, 1), (3, 0, 0, 1), (2, 0, 0, 1))
@@ -63,7 +67,7 @@
     barrier = pltpu.get_barrier_semaphore()
     for offset in partners:
         pl.semaphore_signal(barrier, inc=1, device_id=peer(here, *offset), device_id_type=MESH)
-    pl.semaphore_wait(barrier, len(partners))
+    return lambda: pl.semaphore_wait(barrier, len(partners))
 
 
 def at(index, size, align):
@@ -83,7 +87,7 @@
 
 
 def tiles(width):
-    return [slice(j, j + SUB) for j in range(0, width, SUB)]
+    return [slice(j, min(j + SUB, width)) for j in range(0, width, SUB)]
 
 
 def swap_matrix():
@@ -165,13 +169,19 @@
 ):
     here = place()
     y, z, x, c = here
-    sources = (tok_ref, cot_ref)
     mine = at(c, TOK, TOK)
 
     def cols(k):
         return at(k, FW, 128)
 
-    greet(here, ACROSS + COLUMN)
+    def ecols(k):
+        return at(k, EW, 128)
+
+    met = greet(here, ACROSS + COLUMN)
+    weights = [
+        pltpu.make_async_copy(src, dst, w_sem.at[i])
+        for i, (src, dst) in enumerate(((wg_hbm, wg), (wu_hbm, wu), (wd_hbm, wd)))
+    ]
 
     first = lax.broadcasted_iota(jnp.int32, (8, TOK), 0) == 0
     metas[y, c] = jnp.where(first, routes_ref[...].astype(F32), prob_ref[...])
@@ -182,15 +192,12 @@
             metas.at[y, c], metas.at[y, c], m_s.at[i], m_r.at[i], peer(here, *others[i])
         )
 
-    for i in range(len(others)):
-        meta_copy(i).start()
-
     def yy_copy(k, i):
         return remote(
-            cot_ref.at[:, cols(k)],
+            cot_ref.at[:, ecols(k)],
             raw4.at[k, y, mine, :],
-            yy_s.at[k, i],
-            yy_r.at[k, i],
+            yy_s.at[k],
+            yy_r.at[k],
             peer(here, PLUS_MINUS[i], 0, 0, 0),
         )
 
@@ -198,21 +205,21 @@
         src = (y + PLUS_MINUS[1 - i]) % 4
         half = raw4.at[k, src, pl.ds(pl.multiple_of(c * TOK + i * 64, 64), 64), :]
         return remote(
-            half, half, ff_s.at[k, i], ff_r.at[k, i], peer(here, PLUS_MINUS[i], 0, 0, 0)
+            half, half, ff_s.at[k], ff_r.at[k], peer(here, PLUS_MINUS[i], 0, 0, 0)
         )
 
     def cc_copy(k, i):
         block = raw4.at[k, (y + (3, 1, 2)[i]) % 4, mine, :]
-        return remote(block, block, cc_s.at[k, i], cc_r.at[k, i], peer(here, 0, 0, 0, 1))
+        return remote(block, block, cc_s.at[k], cc_r.at[k], peer(here, 0, 0, 0, 1))
 
     def own_local(k):
         return pltpu.make_async_copy(
-            cot_ref.at[:, cols(k)], raw4.at[k, y, mine, :], own_l.at[k]
+            cot_ref.at[:, ecols(k)], raw4.at[k, y, mine, :], own_l.at[k]
         )
 
     def own_remote(k):
         return remote(
-            cot_ref.at[:, cols(k)],
+            cot_ref.at[:, ecols(k)],
             raw4.at[k, y, mine, :],
             own_s.at[k],
             own_r.at[k],
@@ -223,55 +230,87 @@
         return remote(
             zs4.at[k % 2, :, at((z + d) % 4, BLK, 16), :],
             za4.at[k, :, at(z, BLK, 16), :],
-            zz_s.at[k % 2, d - 1],
-            zz_r.at[k, d - 1],
+            zz_s.at[k % 2],
+            zz_r.at[k],
             peer(here, 0, d, 0, 0),
         )
 
     def xx_copy(k, d):
         return remote(
             xs4.at[k % 2, :, at((x + d) % 4, BLK, 16), :],
-            rows.at[1, :, at(x, BLK, 16), cols(k)],
-            xx_s.at[k % 2, d - 1],
-            xx_r.at[k, d - 1],
+            rows.at[1, :, at(x, BLK, 16), ecols(k)],
+            xx_s.at[k % 2],
+            xx_r.at[k],
             peer(here, 0, 0, d, 0),
         )
 
     def xx_own(k):
         return pltpu.make_async_copy(
             xs4.at[k % 2, :, at(x, BLK, 16), :],
-            rows.at[1, :, at(x, BLK, 16), cols(k)],
+            rows.at[1, :, at(x, BLK, 16), ecols(k)],
             xx_l.at[k % 2],
         )
 
     def stage4_copy(k):
         return pltpu.make_async_copy(
-            rows.at[1, :, :, cols(k)], stage4.at[k % 2], st4_l.at[k % 2]
+            rows.at[1, :, :, ecols(k)], stage4.at[k % 2], st4_l.at[k % 2]
+        )
+
+    def yy_all(k):
+        both = raw4.at[k, pl.ds(0, 2), mine, :]
+        return remote(both, both, yy_s.at[k], yy_r.at[k], peer(here, 1, 0, 0, 0))
+
+    def ff_all(k):
+        both = raw4.at[k, 0, mine, :]
+        return remote(both, both, ff_s.at[k], ff_r.at[k], peer(here, 1, 0, 0, 0))
+
+    def cc_all(k):
+        three = raw4.at[k, pl.ds(0, 3), mine, :]
+        return remote(three, three, cc_s.at[k], cc_r.at[k], peer(here, 0, 0, 0, 1))
+
+    def zz_all(k):
+        return remote(
+            zs4.at[k % 2, :, pl.ds(0, 3 * BLK), :],
+            za4.at[k, :, pl.ds(0, 3 * BLK), :],
+            zz_s.at[k % 2],
+            zz_r.at[k],
+            peer(here, 0, 1, 0, 0),
+        )
+
+    def xx_all(k):
+        return remote(
+            xs4.at[k % 2, :, pl.ds(0, 3 * BLK), :],
+            rows.at[1, :, pl.ds(0, 3 * BLK), ecols(k)],
+            xx_s.at[k % 2],
+            xx_r.at[k],
+            peer(here, 0, 0, 1, 0),
         )
 
     def early_send(k):
         for i in range(2):
             yy_copy(k, i).start()
 
+    def early_own(k):
+        own_local(k).start()
+        own_remote(k).start()
+
     def early_pass(k):
+        yy_all(k).wait_recv()
         for i in range(2):
-            yy_copy(k, i).wait_recv()
             ff_copy(k, i).start()
             cc_copy(k, i).start()
 
     def early_rest(k):
-        for i in range(2):
-            ff_copy(k, i).wait_recv()
+        ff_all(k).wait_recv()
         cc_copy(k, 2).start()
 
     def early_select(k):
         own_local(k).wait()
         own_remote(k).wait()
-        for i in range(3):
-            cc_copy(k, i).wait_recv()
+        cc_all(k).wait_recv()
 
         def block(b, carry):
-            for out in tiles(FW):
+            for out in tiles(EW):
                 picked = nn(sel[b], raw4[k, b, :, out]) * gp[b, :, 0:1]
                 zs4[k % 2, b, :, out] = picked.astype(BF)
             za4[k, b, at(z, BLK, 16), :] = zs4[k % 2, b, at(z, BLK, 16), :]
@@ -282,11 +321,10 @@
             zz_copy(k, d).start()
 
     def early_turn(k):
-        for d in (1, 2, 3):
-            zz_copy(k, d).wait_recv()
+        zz_all(k).wait_recv()
 
         def block(b, carry):
-            for out in tiles(FW):
+            for out in tiles(EW):
                 xs4[k % 2, b, :, out] = nn(perm[...], za4[k, b, :, out]).astype(BF)
             return carry
 
@@ -296,32 +334,26 @@
         xx_own(k).start()
 
     def early_fetch(k):
-        for d in (1, 2, 3):
-            xx_copy(k, d).wait_recv()
+        xx_all(k).wait_recv()
         xx_own(k).wait()
         stage4_copy(k).start()
 
     def early_accumulate(k):
         stage4_copy(k).wait()
-
-        def block(b, carry):
-            acc[2, at(b, ROWS, 16), :] += nt(stage4[k % 2, b], wd[:, cols(k)])
-            return carry
-
-        lax.fori_loop(0, 4, block, 0)
+        acc[2] += nt(stage4[k % 2].reshape(4 * ROWS, EW), wd[:, ecols(k)])
 
     def which(i):
         a = i // FC
-        return a, cols(i - a * (FC - F_EARLY))
-
-    def raw_copies(i):
-        a = i // FC
-        src = sources[a].at[:, cols(i - a * (FC - F_EARLY))]
-        dst = raw.at[i, mine, :]
-        return (
-            pltpu.make_async_copy(src, dst, raw_l.at[i]),
-            remote(src, dst, raw_s.at[i], raw_r.at[i], peer(here, 0, 0, 0, 1)),
-        )
+        return a, cols(i - a * (FC - F_DONE))
+
+    def raw_start(i):
+        def begin(src):
+            dst = raw.at[i, mine, :]
+            pltpu.make_async_copy(src, dst, raw_l.at[i]).start()
+            remote(src, dst, raw_s.at[i], raw_r.at[i], peer(here, 0, 0, 0, 1)).start()
+
+        pl.when(i // FC == 0)(lambda: begin(tok_ref.at[:, cols(i)]))
+        pl.when(i // FC == 1)(lambda: begin(cot_ref.at[:, cols(i - FC + F_DONE)]))
 
     def raw_waits(i):
         src = tok_ref.at[:, cols(0)]
@@ -335,8 +367,8 @@
         return remote(
             zs.at[i % 2, at((z + d) % 4, BLK, 16), :],
             za.at[i, at(z, BLK, 16), :],
-            z_s.at[i % 2, d - 1],
-            z_r.at[i, d - 1],
+            z_s.at[i % 2],
+            z_r.at[i],
             peer(here, 0, d, 0, 0),
         )
 
@@ -345,8 +377,8 @@
         return remote(
             xs.at[i % 2, at((x + d) % 4, BLK, 16), :],
             rows.at[a, y, at(x, BLK, 16), span],
-            x_s.at[i % 2, d - 1],
-            x_r.at[i, d - 1],
+            x_s.at[i % 2],
+            x_r.at[i],
             peer(here, 0, 0, d, 0),
         )
 
@@ -360,17 +392,46 @@
         a, span = which(i)
         block = rows.at[a, y, :, span]
         return remote(
-            block, block, y_s.at[i, p], y_r.at[i, p], peer(here, PLUS_MINUS[p], 0, 0, 0)
+            block, block, y_s.at[i], y_r.at[i], peer(here, PLUS_MINUS[p], 0, 0, 0)
         )
 
     def f_copy(i, p):
         a, span = which(i)
         half = rows.at[a, (y + PLUS_MINUS[1 - p]) % 4, pl.ds(p * 96, 96), span]
-        return remote(half, half, f_s.at[i, p], f_r.at[i, p], peer(here, PLUS_MINUS[p], 0, 0, 0))
+        return remote(half, half, f_s.at[i], f_r.at[i], peer(here, PLUS_MINUS[p], 0, 0, 0))
 
     def stage_copy(i):
         a, span = which(i)
         return pltpu.make_async_copy(rows.at[a, :, :, span], stage.at[i % 2], st_l.at[i % 2])
+
+    def z_all(i):
+        return remote(
+            zs.at[i % 2, pl.ds(0, 3 * BLK), :],
+            za.at[i, pl.ds(0, 3 * BLK), :],
+            z_s.at[i % 2],
+            z_r.at[i],
+            peer(here, 0, 1, 0, 0),
+        )
+
+    def x_all(i):
+        a, span = which(i)
+        return remote(
+            xs.at[i % 2, pl.ds(0, 3 * BLK), :],
+            rows.at[a, y, pl.ds(0, 3 * BLK), span],
+            x_s.at[i % 2],
+            x_r.at[i],
+            peer(here, 0, 0, 1, 0),
+        )
+
+    def y_all(i):
+        a, span = which(i)
+        both = rows.at[a, pl.ds(0, 2), :, span]
+        return remote(both, both, y_s.at[i], y_r.at[i], peer(here, 1, 0, 0, 0))
+
+    def f_all(i):
+        a, span = which(i)
+        both = rows.at[a, y, :, span]
+        return remote(both, both, f_s.at[i], f_r.at[i], peer(here, 1, 0, 0, 0))
 
     def late_select(i):
         for copy in raw_waits(i):
@@ -383,8 +444,7 @@
         za[i, at(z, BLK, 16), :] = zs[i % 2, at(z, BLK, 16), :]
 
     def late_turn(i):
-        for d in (1, 2, 3):
-            z_copy(i, d).wait_recv()
+        z_all(i).wait_recv()
         for out in tiles(FW):
             xs[i % 2, :, out] = nn(perm[...], za[i, :, out]).astype(BF)
         for d in (2, 1, 3):
@@ -392,20 +452,18 @@
         x_own(i).start()
 
     def late_spread(i):
-        for d in (1, 2, 3):
-            x_copy(i, d).wait_recv()
+        x_all(i).wait_recv()
         x_own(i).wait()
         for p in range(2):
             y_copy(i, p).start()
 
     def late_pass(i):
+        y_all(i).wait_recv()
         for p in range(2):
-            y_copy(i, p).wait_recv()
             f_copy(i, p).start()
 
     def late_fetch(i):
-        for p in range(2):
-            f_copy(i, p).wait_recv()
+        f_all(i).wait_recv()
         stage_copy(i).start()
 
     def late_accumulate(i):
@@ -414,45 +472,28 @@
 
         @pl.when(a == 0)
         def _():
-            def block(b, carry):
-                block_rows = at(b, ROWS, 16)
-                tokens = stage[i % 2, b]
-                acc[0, block_rows, :] += nn(tokens, wg[span, :])
-                acc[1, block_rows, :] += nn(tokens, wu[span, :])
-                return carry
-
-            lax.fori_loop(0, 4, block, 0)
+            held = stage[i % 2].reshape(4 * ROWS, FW)
+            acc[0] += nn(held, wg[span, :])
+            acc[1] += nn(held, wu[span, :])
 
         @pl.when(a == 1)
         def _():
-            def block(b, carry):
-                acc[2, at(b, ROWS, 16), :] += nt(stage[i % 2, b], wd[:, span])
-                return carry
-
-            lax.fori_loop(0, 4, block, 0)
-
-    def drain(copy, count, base):
-        def body(k):
-            for i in range(count):
-                copy(k, base + i).wait_send()
-
-        return body
-
+            acc[2] += nt(stage[i % 2].reshape(4 * ROWS, FW), wd[:, span])
+
+    def drain(copy):
+        return lambda k: copy(k).wait_send()
+
+    perm[...] = swap_matrix()
+    acc[...] = jnp.zeros_like(acc)
+    met()
+    for i in range(len(others)):
+        meta_copy(i).start()
     early_send(0)
-    for i in range(F_LATE):
-        for copy in raw_copies(i):
-            copy.start()
-        if i < F_EARLY:
-            own_local(i).start()
-            own_remote(i).start()
-    weights = [
-        pltpu.make_async_copy(src, dst, w_sem.at[i])
-        for i, (src, dst) in enumerate(((wg_hbm, wg), (wu_hbm, wu), (wd_hbm, wd)))
-    ]
+    for i in range(2):
+        raw_start(i)
+    early_own(0)
     for copy in weights:
         copy.start()
-    perm[...] = swap_matrix()
-    acc[...] = jnp.zeros_like(acc)
     for i in range(len(others)):
         meta_copy(i).wait()
 
@@ -483,18 +524,20 @@
     lax.fori_loop(0, 4, plan, 0)
 
     def step(t, carry):
-        when(t - 2, F_LATE, drain(z_copy, 3, 1))
-        when(t - 3, F_LATE, drain(x_copy, 3, 1))
-        when(t - 4, F_LATE, drain(y_copy, 2, 0))
-        when(t - 5, F_LATE, drain(f_copy, 2, 0))
-        when(t - 1, F_EARLY, drain(yy_copy, 2, 0))
-        when(t - 2, F_EARLY, drain(ff_copy, 2, 0))
-        when(t - 3, F_EARLY, drain(cc_copy, 3, 0))
-        when(t - 4, F_EARLY, drain(zz_copy, 3, 1))
-        when(t - 5, F_EARLY, drain(xx_copy, 3, 1))
+        when(t - 2, F_LATE, drain(z_all))
+        when(t - 3, F_LATE, drain(x_all))
+        when(t - 4, F_LATE, drain(y_all))
+        when(t - 5, F_LATE, drain(f_all))
+        when(t - 1, F_EARLY, drain(yy_all))
+        when(t - 2, F_EARLY, drain(ff_all))
+        when(t - 3, F_EARLY, drain(cc_all))
+        when(t - 4, F_EARLY, drain(zz_all))
+        when(t - 5, F_EARLY, drain(xx_all))
 
         when(t, F_LATE, late_select)
         when(t + 1, F_EARLY, early_send)
+        when(t + 1, F_EARLY, early_own)
+        when(t + 2, F_LATE, raw_start)
         when(t, F_EARLY, early_pass)
         when(t - 1, F_LATE, late_turn)
         when(t - 1, F_EARLY, early_rest)
@@ -554,14 +597,12 @@
     xa,
     zs,
     za,
-    cs,
     co,
     cr,
     xs4,
     xa4,
     zs4,
     za4,
-    cs4,
     co4,
     cr4,
     relay4,
@@ -600,12 +641,22 @@
     def cols(k):
         return at(k, BW, 128)
 
+    def ecols(k):
+        return pl.ds(pl.multiple_of(B_FROM + k * CW, 128), CW)
+
     def tile(k, out):
-        return pl.ds(pl.multiple_of(k * BW + out.start, 128), SUB)
-
-    greet(here, ACROSS + COLUMN[:2])
+        return pl.ds(pl.multiple_of(k * BW + out.start, 128), out.stop - out.start)
+
+    def etile(k, out):
+        return pl.ds(pl.multiple_of(B_FROM + k * CW + out.start, 128), out.stop - out.start)
+
+    met = greet(here, ACROSS + COLUMN[:2])
+    spans = ((0, BW), (B_FROM, CW), (BW, B_FROM - BW), (B_FROM + CW, D - B_FROM - CW))
     weights = [
-        pltpu.make_async_copy(src, dst, w_sem.at[i])
+        pltpu.make_async_copy(
+            src.at[pl.ds(first, size)], dst.at[pl.ds(first, size)], w_sem.at[n, i]
+        )
+        for n, (first, size) in enumerate(spans)
         for i, (src, dst) in enumerate(((wg_hbm, wg), (wu_hbm, wu)))
     ]
     for copy in weights:
@@ -620,21 +671,22 @@
         stage_copy(a, 0).start()
     squares[...] = jnp.zeros_like(squares)
     perm[...] = swap_matrix()
-    for copy in weights:
+    met()
+    for copy in weights[:4]:
         copy.wait()
 
-    def partial(block, k, out):
+    def partial(block, span):
         block_rows = at(block, ROWS, 16)
-        total = nt(acts[0, block_rows, :], wg[tile(k, out), :])
-        total = total + nt(acts[1, block_rows, :], wu[tile(k, out), :])
+        total = nt(acts[0, block_rows, :], wg[span, :])
+        total = total + nt(acts[1, block_rows, :], wu[span, :])
         return total.astype(BF)
 
     def p_copy(k, i):
         return remote(
             far.at[k % 2, pl.ds(i * 96, 96), :],
             relay.at[k, i],
-            p_s.at[k % 2, i],
-            p_r.at[k, i],
+            p_s.at[k % 2],
+            p_r.at[k],
             peer(here, PLUS_MINUS[i], 0, 0, 0),
         )
 
@@ -642,8 +694,8 @@
         return remote(
             near.at[i, k % 2],
             summed.at[k, i],
-            n_s.at[k % 2, i],
-            n_r.at[k, i],
+            n_s.at[k % 2],
+            n_r.at[k],
             peer(here, PLUS_MINUS[i], 0, 0, 0),
         )
 
@@ -651,8 +703,8 @@
         return remote(
             xs.at[k % 2, at((x + d) % 4, BLK, 16), :],
             xa.at[k, at(x, BLK, 16), :],
-            x_s.at[k % 2, d - 1],
-            x_r.at[k, d - 1],
+            x_s.at[k % 2],
+            x_r.at[k],
             peer(here, 0, 0, d, 0),
         )
 
@@ -660,36 +712,76 @@
         return remote(
             zs.at[k % 2, at((z + d) % 4, BLK, 16), :],
             za.at[k, at(z, BLK, 16), :],
-            z_s.at[k % 2, d - 1],
-            z_r.at[k, d - 1],
+            z_s.at[k % 2],
+            z_r.at[k],
             peer(here, 0, d, 0, 0),
         )
 
     def c_copy(k):
-        return remote(cs.at[k % 2], cr.at[k], c_s.at[k % 2], c_r.at[k], peer(here, 0, 0, 0, 1))
+        return remote(
+            co.at[k % 2, at(1 - c, TOK, TOK), :],
+            cr.at[k],
+            c_s.at[k % 2],
+            c_r.at[k],
+            peer(here, 0, 0, 0, 1),
+        )
+
+    def whole(src, dst, send, recv):
+        return remote(src, dst, send, recv, peer(here, 1, 0, 0, 0))
+
+    def p_all(k):
+        return whole(far.at[k % 2], relay.at[k], p_s.at[k % 2], p_r.at[k])
+
+    def n_all(k):
+        return whole(near.at[:, k % 2], summed.at[k], n_s.at[k % 2], n_r.at[k])
+
+    def x_all(k):
+        three = pl.ds(0, 3 * BLK)
+        return whole(xs.at[k % 2, three, :], xa.at[k, three, :], x_s.at[k % 2], x_r.at[k])
+
+    def z_all(k):
+        three = pl.ds(0, 3 * BLK)
+        return whole(zs.at[k % 2, three, :], za.at[k, three, :], z_s.at[k % 2], z_r.at[k])
+
+    def xx_all(k):
+        three = pl.ds(0, 3 * BLK)
+        return whole(
+            xs4.at[k % 2, :, three, :], xa4.at[k, :, three, :], xx_s.at[k % 2], xx_r.at[k]
+        )
+
+    def zz_all(k):
+        three = pl.ds(0, 3 * BLK)
+        return whole(
+            zs4.at[k % 2, :, three, :], za4.at[k, :, three, :], zz_s.at[k % 2], zz_r.at[k]
+        )
+
+    def pp_all(k):
+        return whole(cr4.at[k, 0], relay4.at[k], pp_s.at[k], pp_r.at[k])
+
+    def nn_all(k):
+        return whole(cr4.at[k, pl.ds(0, 2)], summed4.at[k], nn_s.at[k], nn_r.at[k])
 
     def late_far(k):
         for out in tiles(BW):
-            far[k % 2, :, out] = partial((y + 2) % 4, k, out)
+            far[k % 2, :, out] = partial((y + 2) % 4, tile(k, out))
         for i in range(2):
             p_copy(k, i).start()
 
     def late_near(k):
+        p_all(k).wait_recv()
         for i in range(2):
-            p_copy(k, i).wait_recv()
             added, plain = slice(i * 96, i * 96 + 96), slice(96 - i * 96, 192 - i * 96)
             for out in tiles(BW):
-                term = partial((y + PLUS_MINUS[i]) % 4, k, out)
+                term = partial((y + PLUS_MINUS[i]) % 4, tile(k, out))
                 both = term[added].astype(F32) + relay[k, i, :, out].astype(F32)
                 near[i, k % 2, added, out] = both.astype(BF)
                 near[i, k % 2, plain, out] = term[plain]
             n_copy(k, i).start()
 
     def late_total(k):
-        for i in range(2):
-            n_copy(k, i).wait_recv()
+        n_all(k).wait_recv()
         for out in tiles(BW):
-            whole = partial(y, k, out).astype(F32)
+            whole = partial(y, tile(k, out)).astype(F32)
             whole = whole + summed[k, 0, :, out].astype(F32)
             whole = whole + summed[k, 1, :, out].astype(F32)
             xs[k % 2, :, out] = whole.astype(BF)
@@ -698,8 +790,7 @@
         xa[k, at(x, BLK, 16), :] = xs[k % 2, at(x, BLK, 16), :]
 
     def late_turn(k):
-        for d in (1, 2, 3):
-            x_copy(k, d).wait_recv()
+        x_all(k).wait_recv()
         for out in tiles(BW):
             zs[k % 2, :, out] = nn(perm[...], xa[k, :, out]).astype(BF)
         for d in (2, 1, 3):
@@ -707,25 +798,23 @@
         za[k, at(z, BLK, 16), :] = zs[k % 2, at(z, BLK, 16), :]
 
     def late_unselect(k):
-        for d in (1, 2, 3):
-            z_copy(k, d).wait_recv()
+        z_all(k).wait_recv()
         for out in tiles(BW):
             block = za[k, :, out]
-            cs[k % 2, :, out] = tn(sel[y, :, at(1 - c, TOK, TOK)], block).astype(BF)
-            co[k % 2, :, out] = tn(sel[y, :, at(c, TOK, TOK)], block).astype(BF)
+            co[k % 2, :, out] = tn(sel[y], block).astype(BF)
         c_copy(k).start()
 
     def late_join(k):
         c_copy(k).wait()
-        whole = co[k % 2].astype(F32) + cr[k].astype(F32)
-        grad_ref[:, cols(k)] = whole.astype(BF)
+        both = co[k % 2, at(c, TOK, TOK), :].astype(F32) + cr[k].astype(F32)
+        grad_ref[:, cols(k)] = both.astype(BF)
 
     def xx_copy(k, d):
         return remote(
             xs4.at[k % 2, :, at((x + d) % 4, BLK, 16), :],
             xa4.at[k, :, at(x, BLK, 16), :],
-            xx_s.at[k % 2, d - 1],
-            xx_r.at[k, d - 1],
+            xx_s.at[k % 2],
+            xx_r.at[k],
             peer(here, 0, 0, d, 0),
         )
 
@@ -733,22 +822,26 @@
         return remote(
             zs4.at[k % 2, :, at((z + d) % 4, BLK, 16), :],
             za4.at[k, :, at(z, BLK, 16), :],
-            zz_s.at[k % 2, d - 1],
-            zz_r.at[k, d - 1],
+            zz_s.at[k % 2],
+            zz_r.at[k],
             peer(here, 0, d, 0, 0),
         )
 
     def cc_copy(k):
         return remote(
-            cs4.at[k % 2], cr4.at[k], cc_s.at[k % 2], cc_r.at[k], peer(here, 0, 0, 0, 1)
+            co4.at[k % 2, :, at(1 - c, TOK, TOK), :],
+            cr4.at[k],
+            cc_s.at[k % 2],
+            cc_r.at[k],
+            peer(here, 0, 0, 0, 1),
         )
 
     def pp_copy(k, i):
         return remote(
             cr4.at[k, (y + 2) % 4, pl.ds(i * 64, 64), :],
             relay4.at[k, i],
-            pp_s.at[k, i],
-            pp_r.at[k, i],
+            pp_s.at[k],
+            pp_r.at[k],
             peer(here, PLUS_MINUS[i], 0, 0, 0),
         )
 
@@ -756,28 +849,25 @@
         return remote(
             cr4.at[k, (y + PLUS_MINUS[i]) % 4],
             summed4.at[k, i],
-            nn_s.at[k, i],
-            nn_r.at[k, i],
+            nn_s.at[k],
+            nn_r.at[k],
             peer(here, PLUS_MINUS[i], 0, 0, 0),
         )
 
     def early_terms(k):
-        def block(b, carry):
-            for out in tiles(BW):
-                xs4[k % 2, b, :, out] = partial(b, k + B_LATE, out)
-            xa4[k, b, at(x, BLK, 16), :] = xs4[k % 2, b, at(x, BLK, 16), :]
-            return carry
-
-        lax.fori_loop(0, 4, block, 0)
+        for out in tiles(CW):
+            span = etile(k, out)
+            term = nt(acts[0], wg[span, :]) + nt(acts[1], wu[span, :])
+            xs4[k % 2, :, :, out] = term.astype(BF).reshape(4, ROWS, out.stop - out.start)
+        xa4[k, :, at(x, BLK, 16), :] = xs4[k % 2, :, at(x, BLK, 16), :]
         for d in (2, 1, 3):
             xx_copy(k, d).start()
 
     def early_turn(k):
-        for d in (1, 2, 3):
-            xx_copy(k, d).wait_recv()
+        xx_all(k).wait_recv()
 
         def block(b, carry):
-            for out in tiles(BW):
+            for out in tiles(CW):
                 zs4[k % 2, b, :, out] = nn(perm[...], xa4[k, b, :, out]).astype(BF)
             za4[k, b, at(z, BLK, 16), :] = zs4[k % 2, b, at(z, BLK, 16), :]
             return carry
@@ -787,14 +877,11 @@
             zz_copy(k, d).start()
 
     def early_unselect(k):
-        for d in (1, 2, 3):
-            zz_copy(k, d).wait_recv()
+        zz_all(k).wait_recv()
 
         def block(b, carry):
-            for out in tiles(BW):
-                whole = za4[k, b, :, out]
-                cs4[k % 2, b, :, out] = tn(sel[b, :, at(1 - c, TOK, TOK)], whole).astype(BF)
-                co4[k % 2, b, :, out] = tn(sel[b, :, at(c, TOK, TOK)], whole).astype(BF)
+            for out in tiles(CW):
+                co4[k % 2, b, :, out] = tn(sel[b], za4[k, b, :, out]).astype(BF)
             return carry
 
         lax.fori_loop(0, 4, block, 0)
@@ -804,8 +891,8 @@
         cc_copy(k).wait()
 
         def block(b, carry):
-            whole = co4[k % 2, b].astype(F32) + cr4[k, b].astype(F32)
-            cr4[k, b] = whole.astype(BF)
+            both = co4[k % 2, b, at(c, TOK, TOK), :].astype(F32) + cr4[k, b].astype(F32)
+            cr4[k, b] = both.astype(BF)
             return carry
 
         lax.fori_loop(0, 4, block, 0)
@@ -813,19 +900,19 @@
             pp_copy(k, i).start()
 
     def early_near(k):
+        pp_all(k).wait_recv()
         for i in range(2):
-            pp_copy(k, i).wait_recv()
             block, added = (y + PLUS_MINUS[i]) % 4, slice(i * 64, i * 64 + 64)
             both = cr4[k, block, added, :].astype(F32) + relay4[k, i].astype(F32)
             cr4[k, block, added, :] = both.astype(BF)
             nn_copy(k, i).start()
 
     def early_join(k):
-        whole = cr4[k, y].astype(F32)
+        nn_all(k).wait()
+        both = cr4[k, y].astype(F32)
         for i in range(2):
-            nn_copy(k, i).wait()
-            whole = whole + summed4[k, i].astype(F32)
-        grad_ref[:, cols(k + B_LATE)] = whole.astype(BF)
+            both = both + summed4[k, i].astype(F32)
+        grad_ref[:, ecols(k)] = both.astype(BF)
 
     def weight_grads(k):
         for a in range(2):
@@ -859,21 +946,22 @@
             out = pl.ds(pl.multiple_of(k * BW + j * 128, 128), 128)
             update_ref[:, out] = (dw[:, out] * squares[...]).astype(BF)
 
-    def drain(copy, count, base):
-        def body(k):
-            for i in range(count):
-                copy(k, base + i).wait_send()
-
-        return body
+    def drain(copy):
+        return lambda k: copy(k).wait_send()
 
     def step(t, carry):
-        when(t - 2, B_LATE, drain(p_copy, 2, 0))
-        when(t - 3, B_LATE, drain(n_copy, 2, 0))
-        when(t - 4, B_LATE, drain(x_copy, 3, 1))
-        when(t - 5, B_LATE, drain(z_copy, 3, 1))
-        when(t - 2, B_EARLY, drain(xx_copy, 3, 1))
-        when(t - 3, B_EARLY, drain(zz_copy, 3, 1))
-        when(t - 5, B_EARLY, drain(pp_copy, 2, 0))
+        when(t - 2, B_LATE, drain(p_all))
+        when(t - 3, B_LATE, drain(n_all))
+        when(t - 4, B_LATE, drain(x_all))
+        when(t - 5, B_LATE, drain(z_all))
+        when(t - 2, B_EARLY, drain(xx_all))
+        when(t - 3, B_EARLY, drain(zz_all))
+        when(t - 5, B_EARLY, drain(pp_all))
+
+        @pl.when(t == 1)
+        def _():
+            for copy in weights[4:]:
+                copy.wait()
 
         when(t, B_LATE, late_far)
         when(t, B_EARLY, early_terms)
@@ -923,12 +1011,12 @@
             held(2, ROWS, FW),
             held(F_LATE, ROWS, FW),
             held(2, ROWS, FW),
-            held(F_EARLY, 4, 2 * TOK, FW),
+            held(F_EARLY, 4, 2 * TOK, EW),
+            held(2, 4, ROWS, EW),
+            held(F_EARLY, 4, ROWS, EW),
+            held(2, 4, ROWS, EW),
             held(2, 4, ROWS, FW),
-            held(F_EARLY, 4, ROWS, FW),
-            held(2, 4, ROWS, FW),
-            held(2, 4, ROWS, FW),
-            held(2, 4, ROWS, FW),
+            held(2, 4, ROWS, EW),
             pltpu.VMEM((3, 4 * ROWS, Q), F32),
             held(D, Q),
             held(D, Q),
@@ -939,29 +1027,29 @@
             dma((F_LATE,)),
             dma((F_LATE,)),
             dma((F_LATE,)),
-            dma((2, 3)),
-            dma((F_LATE, 3)),
-            dma((2, 3)),
-            dma((F_LATE, 3)),
-            dma((2,)),
-            dma((F_LATE, 2)),
-            dma((F_LATE, 2)),
-            dma((F_LATE, 2)),
-            dma((F_LATE, 2)),
+            dma((2,)),
+            dma((F_LATE,)),
+            dma((2,)),
+            dma((F_LATE,)),
+            dma((2,)),
+            dma((F_LATE,)),
+            dma((F_LATE,)),
+            dma((F_LATE,)),
+            dma((F_LATE,)),
             dma((2,)),
             dma((F_EARLY,)),
             dma((F_EARLY,)),
             dma((F_EARLY,)),
-            dma((F_EARLY, 2)),
-            dma((F_EARLY, 2)),
-            dma((F_EARLY, 2)),
-            dma((F_EARLY, 2)),
-            dma((F_EARLY, 3)),
-            dma((F_EARLY, 3)),
-            dma((2, 3)),
-            dma((F_EARLY, 3)),
-            dma((2, 3)),
-            dma((F_EARLY, 3)),
+            dma((F_EARLY,)),
+            dma((F_EARLY,)),
+            dma((F_EARLY,)),
+            dma((F_EARLY,)),
+            dma((F_EARLY,)),
+            dma((F_EARLY,)),
+            dma((2,)),
+            dma((F_EARLY,)),
+            dma((2,)),
+            dma((F_EARLY,)),
             dma((2,)),
             dma((2,)),
         ],
@@ -997,44 +1085,42 @@
             held(B_LATE, ROWS, BW),
             held(2, ROWS, BW),
             held(B_LATE, ROWS, BW),
-            held(2, TOK, BW),
-            held(2, TOK, BW),
+            held(2, 2 * TOK, BW),
             held(B_LATE, TOK, BW),
-            held(2, 4, ROWS, BW),
-            held(B_EARLY, 4, ROWS, BW),
-            held(2, 4, ROWS, BW),
-            held(B_EARLY, 4, ROWS, BW),
-            held(2, 4, TOK, BW),
-            held(2, 4, TOK, BW),
-            held(B_EARLY, 4, TOK, BW),
-            held(B_EARLY, 2, 64, BW),
-            held(B_EARLY, 2, TOK, BW),
+            held(2, 4, ROWS, CW),
+            held(B_EARLY, 4, ROWS, CW),
+            held(2, 4, ROWS, CW),
+            held(B_EARLY, 4, ROWS, CW),
+            held(2, 4, 2 * TOK, CW),
+            held(B_EARLY, 4, TOK, CW),
+            held(B_EARLY, 2, 64, CW),
+            held(B_EARLY, 2, TOK, CW),
             held(2, 2, 4, ROWS, BW),
             pltpu.VMEM((Q, D), F32),
             pltpu.VMEM((Q, 128), F32),
             held(D, Q),
             held(D, Q),
-            dma((2,)),
-            dma((2, 2)),
-            dma((B_LATE, 2)),
-            dma((2, 2)),
-            dma((B_LATE, 2)),
-            dma((2, 3)),
-            dma((B_LATE, 3)),
-            dma((2, 3)),
-            dma((B_LATE, 3)),
+            dma((4, 2)),
             dma((2,)),
             dma((B_LATE,)),
-            dma((2, 3)),
-            dma((B_EARLY, 3)),
-            dma((2, 3)),
-            dma((B_EARLY, 3)),
+            dma((2,)),
+            dma((B_LATE,)),
+            dma((2,)),
+            dma((B_LATE,)),
+            dma((2,)),
+            dma((B_LATE,)),
+            dma((2,)),
+            dma((B_LATE,)),
             dma((2,)),
             dma((B_EARLY,)),
-            dma((B_EARLY, 2)),
-            dma((B_EARLY, 2)),
-            dma((B_EARLY, 2)),
-            dma((B_EARLY, 2)),
+            dma((2,)),
+            dma((B_EARLY,)),
+            dma((2,)),
+            dma((B_EARLY,)),
+            dma((B_EARLY,)),
+            dma((B_EARLY,)),
+            dma((B_EARLY,)),
+            dma((B_EARLY,)),
             dma((2, 2)),
         ],
         compiler_params=pltpu.CompilerParams(

time: 312 us -> 280 us (0.90)
  Pallas kernels: 304 us -> 274 us
    pallas_call x1, Pallas kernels: 193 us -> 177 us  [shards(): pl.pallas_call(forward_kernel, name='dispatch', out_shape=(jax.ShapeDtype...]
    pallas_call x1, Pallas kernels: 111 us -> 96.4 us  [shards(): pl.pallas_call(backward_kernel, name='combine', out_shape=(jax.ShapeDtype...]
where the time goes in v3:
time: 280 us
  Pallas kernels  274 us (98%)
  local copies, waits for them, and re-layouts  5.4 us (2%)
    pallas_call x1, Pallas kernels, shards(): pl.pallas_call(forward_kernel, name='dispatch', out_shape=(jax.ShapeDtype...  177 us
    pallas_call x1, Pallas kernels, shards(): pl.pallas_call(backward_kernel, name='combine', out_shape=(jax.ShapeDtype...  96.4 us

profile of v3, /device:TPU:0, one launch (start us, length us, event | category | flops | bytes accessed | tf_op | source)
XLA Modules:
  0.0 280.0 jit_solution(11569592754435625992)
XLA Ops:
  0.6 177.5 %dispatch.1 = (bf16[2,4,192,7168]{3,2,1,0:T(8,128)(2,1)}, bf16[2,768,256]{2,1,0:T(8,128)(2,1)}, bf16[3,256,768]{2,1,0:T(8,128)(2,1)}, bf16[4,192,256]{2,1,0:T(8,128)(2,1)}) custom-call(s32[1,128]{1,0:T(1,128)} %bitcast.12, f32[1,128]{1,0:T(1,128)} %bitcast.13, bf16[128,7168]{1,0:T(8,128)(2,1)} %tok_ref.1, bf16[128,7168]{1,0:T(8,128)(2,1)} %cot_ref.1, ...), custom_call_target="tpu_custom_call" | custom-call | tf_op jit(solution)/shard_map/dispatch/pallas_call | solution.py:995
  178.1 96.4 %combine.1 = (bf16[128,7168]{1,0:T(8,128)(2,1)}, bf16[256,7168]{1,0:T(8,128)(2,1)}, f32[1,256]{1,0:T(1,128)}) custom-call(bf16[2,768,256]{2,1,0:T(8,128)(2,1)} %get-tuple-element.10.acts, bf16[3,256,768]{2,1,0:T(8,128)(2,1)} %get-tuple-element.11.acts_t, bf16[4,192,256]{2,1,0:T(8,128)(2,1)} %get-tuple-element.12.sel, ...), custom_call_target="tpu_custom_call" | custom-call | tf_op jit(solution)/shard_map/combine/pallas_call | solution.py:1068
  274.6 0.0 copy-start
  274.6 3.0 %copy.14 = bf16[128,7168]{1,0:T(8,128)(2,1)} copy(bf16[128,7168]{1,0:T(8,128)(2,1)} %get-tuple-element.20) | data formatting | bytes 3670016
  277.6 0.0 copy-done
  277.6 0.0 copy-start.1
  277.6 1.8 copy.15
  279.4 0.0 copy-done.1
  279.4 0.6 copy.16
Async XLA Ops:
  274.6 3.0 %copy-start = (bf16[256,7168]{1,0:T(8,128)(2,1)S(1)}, bf16[256,7168]{1,0:T(8,128)(2,1)}, u32[]{:S(2)}) copy-start(bf16[256,7168]{1,0:T(8,128)(2,1)} %get-tuple-element.15) | copy-start | bytes 11010052
  277.6 1.8 copy-start.1

commit v4 on v3

--- a/solution.py
+++ b/solution.py
@@ -116,7 +116,6 @@
     wd_hbm,
     rows,
     acts,
-    acts_t,
     sel,
     metas,
     gp,
@@ -489,9 +488,11 @@
     for i in range(len(others)):
         meta_copy(i).start()
     early_send(0)
+    early_send(1)
     for i in range(2):
         raw_start(i)
     early_own(0)
+    early_own(1)
     for copy in weights:
         copy.start()
     for i in range(len(others)):
@@ -528,35 +529,36 @@
         when(t - 3, F_LATE, drain(x_all))
         when(t - 4, F_LATE, drain(y_all))
         when(t - 5, F_LATE, drain(f_all))
-        when(t - 1, F_EARLY, drain(yy_all))
-        when(t - 2, F_EARLY, drain(ff_all))
-        when(t - 3, F_EARLY, drain(cc_all))
-        when(t - 4, F_EARLY, drain(zz_all))
-        when(t - 5, F_EARLY, drain(xx_all))
+        when(t, F_EARLY, drain(yy_all))
+        when(t - 1, F_EARLY, drain(ff_all))
+        when(t - 2, F_EARLY, drain(cc_all))
+        when(t - 3, F_EARLY, drain(zz_all))
+        when(t - 4, F_EARLY, drain(xx_all))
 
         when(t, F_LATE, late_select)
-        when(t + 1, F_EARLY, early_send)
-        when(t + 1, F_EARLY, early_own)
+        when(t + 2, F_EARLY, early_send)
+        when(t + 2, F_EARLY, early_own)
         when(t + 2, F_LATE, raw_start)
-        when(t, F_EARLY, early_pass)
+        when(t + 1, F_EARLY, early_pass)
         when(t - 1, F_LATE, late_turn)
-        when(t - 1, F_EARLY, early_rest)
+        when(t, F_EARLY, early_rest)
         when(t - 2, F_LATE, late_spread)
-        when(t - 2, F_EARLY, early_select)
+        when(t - 1, F_EARLY, early_select)
         when(t - 3, F_LATE, late_pass)
-        when(t - 3, F_EARLY, early_turn)
+        when(t - 2, F_EARLY, early_turn)
         when(t - 4, F_LATE, late_fetch)
-        when(t - 4, F_EARLY, early_fetch)
-
-        @pl.when(t == 5)
+        when(t - 3, F_EARLY, early_fetch)
+
+        @pl.when(t == 4)
         def _():
             for copy in weights:
                 copy.wait()
 
         when(t - 5, F_LATE, late_accumulate)
-        when(t - 5, F_EARLY, early_accumulate)
+        when(t - 4, F_EARLY, early_accumulate)
         return carry
 
+    early_pass(0)
     lax.fori_loop(0, F_LATE + 5, step, 0)
 
     def finish(b, carry):
@@ -569,9 +571,7 @@
         up_grad = grad * silu
         acts[0, part, :] = gate_grad.astype(BF)
         acts[1, part, :] = up_grad.astype(BF)
-        acts_t[0, :, part] = hidden.T.astype(BF)
-        acts_t[1, :, part] = gate_grad.T.astype(BF)
-        acts_t[2, :, part] = up_grad.T.astype(BF)
+        acts[2, part, :] = hidden.astype(BF)
         return carry
 
     lax.fori_loop(0, 3, finish, 0)
@@ -579,15 +579,17 @@
 
 def backward_kernel(
     acts,
-    acts_t,
     sel,
     rows,
     wg_hbm,
     wu_hbm,
     moment_ref,
+    grad_hbm,
+    update_hbm,
+    second_ref,
+    acts_t,
     grad_ref,
     update_ref,
-    second_ref,
     perm,
     far,
     relay,
@@ -634,12 +636,19 @@
     nn_s,
     nn_r,
     st_l,
+    out_l,
 ):
     here = place()
     y, z, x, c = here
 
     def cols(k):
         return at(k, BW, 128)
+
+    def grad_out(span):
+        return pltpu.make_async_copy(grad_ref.at[:, span], grad_hbm.at[:, span], out_l.at[0])
+
+    def update_out(span):
+        return pltpu.make_async_copy(update_ref.at[:, span], update_hbm.at[:, span], out_l.at[1])
 
     def ecols(k):
         return pl.ds(pl.multiple_of(B_FROM + k * CW, 128), CW)
@@ -808,6 +817,7 @@
         c_copy(k).wait()
         both = co[k % 2, at(c, TOK, TOK), :].astype(F32) + cr[k].astype(F32)
         grad_ref[:, cols(k)] = both.astype(BF)
+        grad_out(cols(k)).start()
 
     def xx_copy(k, d):
         return remote(
@@ -913,6 +923,16 @@
         for i in range(2):
             both = both + summed4[k, i].astype(F32)
         grad_ref[:, ecols(k)] = both.astype(BF)
+        grad_out(ecols(k)).start()
+
+    def turn_acts():
+        def block(b, carry):
+            part = at(b, Q, 256)
+            for n, source in enumerate((2, 0, 1)):
+                acts_t[n, :, part] = acts[source, part, :].astype(F32).T.astype(BF)
+            return carry
+
+        lax.fori_loop(0, 3, block, 0)
 
     def weight_grads(k):
         for a in range(2):
@@ -945,6 +965,7 @@
         for j in range(BW // 128):
             out = pl.ds(pl.multiple_of(k * BW + j * 128, 128), 128)
             update_ref[:, out] = (dw[:, out] * squares[...]).astype(BF)
+        update_out(cols(k)).start()
 
     def drain(copy):
         return lambda k: copy(k).wait_send()
@@ -975,6 +996,7 @@
         when(t - 4, B_EARLY, early_near)
         when(t - 5, B_LATE, late_join)
         when(t - 5, B_EARLY, early_join)
+        pl.when(t == 0)(turn_acts)
         for n in range(2):
             when(t * 2 + n, BC, weight_grads)
         for n in range(3):
@@ -982,6 +1004,8 @@
         return carry
 
     lax.fori_loop(0, B_LATE + 5, step, 0)
+    grad_out(pl.ds(0, D)).wait()
+    update_out(pl.ds(0, D)).wait()
 
 
 def shards(tokens, grad_out, routes, gate_prob, w_gate, w_up, w_down, moment_prev):
@@ -992,17 +1016,16 @@
     def held(*shape):
         return pltpu.VMEM(shape, BF)
 
-    rows, acts, acts_t, sel = pl.pallas_call(
+    rows, acts, sel = pl.pallas_call(
         forward_kernel,
         name="dispatch",
         out_shape=(
             jax.ShapeDtypeStruct((2, 4, ROWS, D), BF),
-            jax.ShapeDtypeStruct((2, 4 * ROWS, Q), BF),
-            jax.ShapeDtypeStruct((3, Q, 4 * ROWS), BF),
+            jax.ShapeDtypeStruct((3, 4 * ROWS, Q), BF),
             jax.ShapeDtypeStruct((4, ROWS, 2 * TOK), BF),
         ),
         in_specs=[vmem, vmem, hbm, hbm, hbm, hbm, hbm],
-        out_specs=(hbm, vmem, vmem, vmem),
+        out_specs=(hbm, vmem, vmem),
         scratch_shapes=[
             pltpu.VMEM((4, 2, 8, TOK), F32),
             pltpu.VMEM((4, ROWS, 128), F32),
@@ -1073,9 +1096,12 @@
             jax.ShapeDtypeStruct((Q, D), BF),
             jax.ShapeDtypeStruct((1, Q), F32),
         ),
-        in_specs=[vmem, vmem, vmem, hbm, hbm, hbm, vmem],
-        out_specs=(vmem, vmem, vmem),
+        in_specs=[vmem, vmem, hbm, hbm, hbm, vmem],
+        out_specs=(hbm, hbm, vmem),
         scratch_shapes=[
+            held(3, Q, 4 * ROWS),
+            held(TOK, D),
+            held(Q, D),
             held(ROWS, ROWS),
             held(2, ROWS, BW),
             held(B_LATE, 2, 96, BW),
@@ -1122,11 +1148,12 @@
             dma((B_EARLY,)),
             dma((B_EARLY,)),
             dma((2, 2)),
+            dma((2,)),
         ],
         compiler_params=pltpu.CompilerParams(
             collective_id=1, has_side_effects=True, vmem_limit_bytes=60 * 2**20
         ),
-    )(acts, acts_t, sel, rows, w_gate[0], w_up[0], moment_prev)
+    )(acts, sel, rows, w_gate[0], w_up[0], moment_prev)
     return grad_in, update[None], second
 
 

time: 280 us -> 276 us (0.986)
  Pallas kernels: 274 us -> 269 us
    pallas_call x1, Pallas kernels: 177 us -> 174 us  [shards(): pl.pallas_call(forward_kernel, name='dispatch', out_shape=(jax.ShapeDtype...]
where the time goes in v4:
time: 276 us; the launch traced here: 275 us
  Pallas kernels  269 us (97%)
  local copies, waits for them, and re-layouts  5.4 us (2%)
    pallas_call x1, Pallas kernels, shards(): pl.pallas_call(forward_kernel, name='dispatch', out_shape=(jax.ShapeDtype...  174 us
    pallas_call x1, Pallas kernels, shards(): pl.pallas_call(backward_kernel, name='combine', out_shape=(jax.ShapeDtype...  95.6 us

profile of v4, /device:TPU:0, one launch (start us, length us, event | category | flops | bytes accessed | tf_op | source)
XLA Modules:
  0.0 275.3 jit_solution(2660784270689142412)
XLA Ops:
  0.6 173.7 %dispatch.1 = (bf16[2,4,192,7168]{3,2,1,0:T(8,128)(2,1)}, bf16[3,768,256]{2,1,0:T(8,128)(2,1)}, bf16[4,192,256]{2,1,0:T(8,128)(2,1)}) custom-call(s32[1,128]{1,0:T(1,128)} %bitcast.12, f32[1,128]{1,0:T(1,128)} %bitcast.13, bf16[128,7168]{1,0:T(8,128)(2,1)} %tok_ref.1, bf16[128,7168]{1,0:T(8,128)(2,1)} %cot_ref.1, bf16[7168,256]{1,0:T(8,128)(2,1)} %bitcast.6, ...), custom_call_target="tpu_custom_call" | custom-call | tf_op jit(solution)/shard_map/dispatch/pallas_call | solution.py:1019
  174.3 95.6 %combine.1 = (bf16[128,7168]{1,0:T(8,128)(2,1)}, bf16[256,7168]{1,0:T(8,128)(2,1)}, f32[1,256]{1,0:T(1,128)}) custom-call(bf16[3,768,256]{2,1,0:T(8,128)(2,1)} %get-tuple-element.9.acts, bf16[4,192,256]{2,1,0:T(8,128)(2,1)} %get-tuple-element.10.sel, bf16[2,4,192,7168]{3,2,1,0:T(8,128)(2,1)} %get-tuple-element.11.rows, bf16[7168,256]{1,0:T(8,128)(2,1)} %bitcast.7, ...), custom_call_target="tpu_custom_call" | custom-call | tf_op jit(solution)/shard_map/combine/pallas_call | solution.py:1091
  269.9 0.0 copy-start
  269.9 3.0 %copy.14 = bf16[128,7168]{1,0:T(8,128)(2,1)} copy(bf16[128,7168]{1,0:T(8,128)(2,1)} %get-tuple-element.18) | data formatting | bytes 3670016
  272.9 0.0 copy-done
  272.9 0.0 copy-start.1
  272.9 1.8 copy.15
  274.7 0.0 copy-done.1
  274.7 0.6 copy.16
Async XLA Ops:
  269.9 3.0 %copy-start = (bf16[256,7168]{1,0:T(8,128)(2,1)S(1)}, bf16[256,7168]{1,0:T(8,128)(2,1)}, u32[]{:S(2)}) copy-start(bf16[256,7168]{1,0:T(8,128)(2,1)} %get-tuple-element.13) | copy-start | bytes 11010052
  272.9 1.8 copy-start.1

commit v5 on v4

--- a/solution.py
+++ b/solution.py
@@ -528,7 +528,6 @@
         when(t - 2, F_LATE, drain(z_all))
         when(t - 3, F_LATE, drain(x_all))
         when(t - 4, F_LATE, drain(y_all))
-        when(t - 5, F_LATE, drain(f_all))
         when(t, F_EARLY, drain(yy_all))
         when(t - 1, F_EARLY, drain(ff_all))
         when(t - 2, F_EARLY, drain(cc_all))
@@ -547,6 +546,7 @@
         when(t - 3, F_LATE, late_pass)
         when(t - 2, F_EARLY, early_turn)
         when(t - 4, F_LATE, late_fetch)
+        when(t - 4, F_LATE, drain(f_all))
         when(t - 3, F_EARLY, early_fetch)
 
         @pl.when(t == 4)
@@ -554,12 +554,12 @@
             for copy in weights:
                 copy.wait()
 
-        when(t - 5, F_LATE, late_accumulate)
         when(t - 4, F_EARLY, early_accumulate)
+        when(t - 4, F_LATE, late_accumulate)
         return carry
 
     early_pass(0)
-    lax.fori_loop(0, F_LATE + 5, step, 0)
+    lax.fori_loop(0, F_LATE + 4, step, 0)
 
     def finish(b, carry):
         part = at(b, Q, 256)
@@ -985,20 +985,20 @@
                 copy.wait()
 
         when(t, B_LATE, late_far)
+        when(t - 1, B_LATE, late_near)
         when(t, B_EARLY, early_terms)
-        when(t - 1, B_LATE, late_near)
+        pl.when(t == 0)(turn_acts)
+        when(t * 2, BC, weight_grads)
         when(t - 1, B_EARLY, early_turn)
         when(t - 2, B_LATE, late_total)
         when(t - 2, B_EARLY, early_unselect)
         when(t - 3, B_LATE, late_turn)
+        when(t * 2 + 1, BC, weight_grads)
         when(t - 3, B_EARLY, early_far)
         when(t - 4, B_LATE, late_unselect)
         when(t - 4, B_EARLY, early_near)
         when(t - 5, B_LATE, late_join)
         when(t - 5, B_EARLY, early_join)
-        pl.when(t == 0)(turn_acts)
-        for n in range(2):
-            when(t * 2 + n, BC, weight_grads)
         for n in range(3):
             when((t - BC // 2) * 3 + n, BC, update)
         return carry

time: 276 us -> 274 us (level)
  no operation moved by 1% of the time
where the time goes in v5:
time: 274 us; the launch traced here: 273 us
  Pallas kernels  267 us (97%)
  local copies, waits for them, and re-layouts  5.4 us (2%)
    pallas_call x1, Pallas kernels, shards(): pl.pallas_call(forward_kernel, name='dispatch', out_shape=(jax.ShapeDtype...  174 us
    pallas_call x1, Pallas kernels, shards(): pl.pallas_call(backward_kernel, name='combine', out_shape=(jax.ShapeDtype...  93.9 us

profile of v5, /device:TPU:0, one launch (start us, length us, event | category | flops | bytes accessed | tf_op | source)
XLA Modules:
  0.0 273.4 jit_solution(12915756804441688337)
XLA Ops:
  0.6 173.5 %dispatch.1 = (bf16[2,4,192,7168]{3,2,1,0:T(8,128)(2,1)}, bf16[3,768,256]{2,1,0:T(8,128)(2,1)}, bf16[4,192,256]{2,1,0:T(8,128)(2,1)}) custom-call(s32[1,128]{1,0:T(1,128)} %bitcast.12, f32[1,128]{1,0:T(1,128)} %bitcast.13, bf16[128,7168]{1,0:T(8,128)(2,1)} %tok_ref.1, bf16[128,7168]{1,0:T(8,128)(2,1)} %cot_ref.1, bf16[7168,256]{1,0:T(8,128)(2,1)} %bitcast.6, ...), custom_call_target="tpu_custom_call" | custom-call | tf_op jit(solution)/shard_map/dispatch/pallas_call | solution.py:1019
  174.2 93.9 %combine.1 = (bf16[128,7168]{1,0:T(8,128)(2,1)}, bf16[256,7168]{1,0:T(8,128)(2,1)}, f32[1,256]{1,0:T(1,128)}) custom-call(bf16[3,768,256]{2,1,0:T(8,128)(2,1)} %get-tuple-element.9.acts, bf16[4,192,256]{2,1,0:T(8,128)(2,1)} %get-tuple-element.10.sel, bf16[2,4,192,7168]{3,2,1,0:T(8,128)(2,1)} %get-tuple-element.11.rows, bf16[7168,256]{1,0:T(8,128)(2,1)} %bitcast.7, ...), custom_call_target="tpu_custom_call" | custom-call | tf_op jit(solution)/shard_map/combine/pallas_call | solution.py:1091
  268.0 0.0 copy-start
  268.0 3.0 %copy.14 = bf16[128,7168]{1,0:T(8,128)(2,1)} copy(bf16[128,7168]{1,0:T(8,128)(2,1)} %get-tuple-element.18) | data formatting | bytes 3670016
  271.0 0.0 copy-done
  271.0 0.0 copy-start.1
  271.0 1.8 copy.15
  272.9 0.0 copy-done.1
  272.9 0.6 copy.16
Async XLA Ops:
  268.0 3.0 %copy-start = (bf16[256,7168]{1,0:T(8,128)(2,1)S(1)}, bf16[256,7168]{1,0:T(8,128)(2,1)}, u32[]{:S(2)}) copy-start(bf16[256,7168]{1,0:T(8,128)(2,1)} %get-tuple-element.13) | copy-start | bytes 11010052
  271.0 1.8 copy-start.1

commit v6 on v5

--- a/solution.py
+++ b/solution.py
@@ -541,10 +541,10 @@
         when(t + 1, F_EARLY, early_pass)
         when(t - 1, F_LATE, late_turn)
         when(t, F_EARLY, early_rest)
+        when(t - 1, F_EARLY, early_select)
         when(t - 2, F_LATE, late_spread)
-        when(t - 1, F_EARLY, early_select)
+        when(t - 2, F_EARLY, early_turn)
         when(t - 3, F_LATE, late_pass)
-        when(t - 2, F_EARLY, early_turn)
         when(t - 4, F_LATE, late_fetch)
         when(t - 4, F_LATE, drain(f_all))
         when(t - 3, F_EARLY, early_fetch)

time: 274 us -> 274 us (level)
  no operation moved by 1% of the time
where the time goes in v6:
time: 274 us; the launch traced here: 273 us
  Pallas kernels  267 us (97%)
  local copies, waits for them, and re-layouts  5.4 us (2%)
    pallas_call x1, Pallas kernels, shards(): pl.pallas_call(forward_kernel, name='dispatch', out_shape=(jax.ShapeDtype...  173 us
    pallas_call x1, Pallas kernels, shards(): pl.pallas_call(backward_kernel, name='combine', out_shape=(jax.ShapeDtype...  94.4 us

profile of v6, /device:TPU:0, one launch (start us, length us, event | category | flops | bytes accessed | tf_op | source)
XLA Modules:
  0.0 273.3 jit_solution(5899708753545577071)
XLA Ops:
  0.6 172.8 %dispatch.1 = (bf16[2,4,192,7168]{3,2,1,0:T(8,128)(2,1)}, bf16[3,768,256]{2,1,0:T(8,128)(2,1)}, bf16[4,192,256]{2,1,0:T(8,128)(2,1)}) custom-call(s32[1,128]{1,0:T(1,128)} %bitcast.12, f32[1,128]{1,0:T(1,128)} %bitcast.13, bf16[128,7168]{1,0:T(8,128)(2,1)} %tok_ref.1, bf16[128,7168]{1,0:T(8,128)(2,1)} %cot_ref.1, bf16[7168,256]{1,0:T(8,128)(2,1)} %bitcast.6, ...), custom_call_target="tpu_custom_call" | custom-call | tf_op jit(solution)/shard_map/dispatch/pallas_call | solution.py:1019
  173.4 94.4 %combine.1 = (bf16[128,7168]{1,0:T(8,128)(2,1)}, bf16[256,7168]{1,0:T(8,128)(2,1)}, f32[1,256]{1,0:T(1,128)}) custom-call(bf16[3,768,256]{2,1,0:T(8,128)(2,1)} %get-tuple-element.9.acts, bf16[4,192,256]{2,1,0:T(8,128)(2,1)} %get-tuple-element.10.sel, bf16[2,4,192,7168]{3,2,1,0:T(8,128)(2,1)} %get-tuple-element.11.rows, bf16[7168,256]{1,0:T(8,128)(2,1)} %bitcast.7, ...), custom_call_target="tpu_custom_call" | custom-call | tf_op jit(solution)/shard_map/combine/pallas_call | solution.py:1091
  267.9 0.0 copy-start
  267.9 3.0 %copy.14 = bf16[128,7168]{1,0:T(8,128)(2,1)} copy(bf16[128,7168]{1,0:T(8,128)(2,1)} %get-tuple-element.18) | data formatting | bytes 3670016
  270.9 0.0 copy-done
  270.9 0.0 copy-start.1
  270.9 1.8 copy.15
  272.7 0.0 copy-done.1
  272.7 0.6 copy.16
Async XLA Ops:
  267.9 3.0 %copy-start = (bf16[256,7168]{1,0:T(8,128)(2,1)S(1)}, bf16[256,7168]{1,0:T(8,128)(2,1)}, u32[]{:S(2)}) copy-start(bf16[256,7168]{1,0:T(8,128)(2,1)} %get-tuple-element.13) | copy-start | bytes 11010052
  270.9 1.8 copy-start.1
